TPU v7x, 128 devices: a whole 4x4x4 slice. The times are simulated.
128 devices in a mesh: tile: 32 (over x, z_lo, y), mode: 4 (over z_hi, core).
Axes of the slice: x: 4, y: 4, z: 4 (z_hi: 2, z_lo: 2; z = z_hi * 2 + z_lo), core: 2. Of those that a mesh axis runs over, the one named last changes fastest.
Arguments:
- object_phase: float32 [2, 8192, 512], P(None, 'tile'), may hold values from -3.140625 to 3.140625
- object_absorb: float32 [2, 8192, 512], P(None, 'tile'), may hold values from 0 to 0.5
- probe_modes: float32 [8, 2, 256, 256], P('mode'), may hold values from -6 to 6
- measured: float32 [64, 256, 256], P('tile'), may hold values from 0.5 to 50
- offsets: int32 [64, 2], P('tile'), may hold values from 0 to 256, as said below
- counts: int32 [32], P('tile'), may hold values from 1 to 2, as said below
Outputs:
- grad_phase: float32 [2, 8192, 512], P(None, 'tile', 'mode')
- grad_absorb: float32 [2, 8192, 512], P(None, 'tile', 'mode')
- grad_probe: float32 [8, 2, 256, 256], P('mode')
Inputs may be any that keep to these rules, and one draw needn't show every extreme that they name: offsets[p, 0] is below 256 and offsets[p, 1] at most 256, so each patch lies inside its strip's columns and reaches at most 255 rows into the next strip. The first counts[t] slots of tile t are in use, the others are not.
All inputs are finite; a program needn't handle non-finite values.
Results may differ from a plain program's by a relative error of at most 0.0003.
Values sent between devices are 32-bit elements; how exact they have to be, the bound alone decides.
No kernel may reach another device: no remote copies, remote signals or barrier semaphores. Data moves between devices by JAX's collectives and lax.ppermute only.
A program may use at most 128 MiB of HBM per device.

v0:
```python
import math

import jax
import jax.numpy as jnp
from jax import lax
from jax.sharding import PartitionSpec as P

fresnel_number = 40.0


def shifted(block, axis, distance):
    devices = range(lax.axis_size(axis))
    route = [(i - distance, i) for i in devices if i - distance in devices]
    return lax.ppermute(block, axis, route)


def propagator(length):
    counter = jnp.arange(length, dtype=jnp.int32)
    freq = ((counter + length // 2) % length - length // 2).astype(jnp.float32) / length
    radial = freq[:, None] ** 2 + freq[None, :] ** 2
    angle_map = -math.pi * fresnel_number * radial
    return (jnp.cos(angle_map), jnp.sin(angle_map))


def dft_tables(length):
    counter = jnp.arange(length, dtype=jnp.int32)
    product = counter[:, None] * counter[None, :] % length
    angle_map = 2.0 * math.pi / length * product.astype(jnp.float32)
    norm_scale = 1.0 / math.sqrt(length)
    return (jnp.cos(angle_map) * norm_scale, -jnp.sin(angle_map) * norm_scale)


def left_apply(matrix, field):
    return jnp.einsum("kn,...nm->...km", matrix, field, precision=lax.Precision.HIGHEST)


def right_apply(field, matrix):
    return jnp.einsum("...km,ml->...kl", field, matrix, precision=lax.Precision.HIGHEST)


def transform(field_real, field_imag, table_real, table_imag):
    mid_real = left_apply(table_real, field_real) - left_apply(table_imag, field_imag)
    mid_imag = left_apply(table_real, field_imag) + left_apply(table_imag, field_real)
    out_real = right_apply(mid_real, table_real) - right_apply(mid_imag, table_imag)
    out_imag = right_apply(mid_real, table_imag) + right_apply(mid_imag, table_real)
    return (out_real, out_imag)


def multiply(first_real, first_imag, second_real, second_imag):
    return (
        first_real * second_real - first_imag * second_imag,
        first_real * second_imag + first_imag * second_real,
    )


def far_field(patch_phase, patch_absorb, probe_modes):
    length = probe_modes.shape[-1]
    table_real, table_imag = dft_tables(length)
    kernel_real, kernel_imag = propagator(length)
    magnitude = jnp.exp(-patch_absorb)
    trans_real = magnitude * jnp.cos(patch_phase)
    trans_imag = magnitude * jnp.sin(patch_phase)
    wave_real, wave_imag = multiply(
        probe_modes[None, :, 0],
        probe_modes[None, :, 1],
        trans_real[:, None, 0],
        trans_imag[:, None, 0],
    )
    spec_real, spec_imag = transform(wave_real, wave_imag, table_real, table_imag)
    spec_real, spec_imag = multiply(spec_real, spec_imag, kernel_real, kernel_imag)
    wave_real, wave_imag = transform(spec_real, spec_imag, table_real, -table_imag)
    wave_real, wave_imag = multiply(
        wave_real, wave_imag, trans_real[:, None, 1], trans_imag[:, None, 1]
    )
    return transform(wave_real, wave_imag, table_real, table_imag)


def amplitude(intensity, target, valid):
    return valid * (1.0 - jnp.sqrt(target + 1.0) / jnp.sqrt(intensity + 1.0))


def per_device(object_phase, object_absorb, probe_modes, measured, offsets, counts):
    layers, strip, columns = object_phase.shape
    length = probe_modes.shape[-1]
    slots = measured.shape[0]
    below_phase, below_absorb = shifted((object_phase, object_absorb), "tile", -1)
    ext_phase = jnp.concatenate([object_phase, below_phase], axis=1)
    ext_absorb = jnp.concatenate([object_absorb, below_absorb], axis=1)
    valid = (jnp.arange(slots, dtype=jnp.int32) < counts[0]).astype(jnp.float32)
    patch_shape = (layers, length, length)

    def cut_patch(source, corner):
        return lax.dynamic_slice(source, (jnp.int32(0), corner[0], corner[1]), patch_shape)

    patch_phase = jax.vmap(cut_patch, in_axes=(None, 0))(ext_phase, offsets)
    patch_absorb = jax.vmap(cut_patch, in_axes=(None, 0))(ext_absorb, offsets)
    field, pullback = jax.vjp(far_field, patch_phase, patch_absorb, probe_modes)
    field_real, field_imag = field
    partial_intensity = jnp.sum(field_real * field_real + field_imag * field_imag, axis=1)
    total = lax.psum(partial_intensity, "mode")
    factor = amplitude(total, measured, valid[:, None, None])
    grad_patch_phase, grad_patch_absorb, grad_probe = pullback(
        (factor[:, None] * field_real, factor[:, None] * field_imag)
    )

    def deposit(slot_index, totals):
        total_phase, total_absorb = totals
        corner = (jnp.int32(0), offsets[slot_index, 0], offsets[slot_index, 1])
        total_phase = lax.dynamic_update_slice(
            total_phase,
            lax.dynamic_slice(total_phase, corner, patch_shape) + grad_patch_phase[slot_index],
            corner,
        )
        total_absorb = lax.dynamic_update_slice(
            total_absorb,
            lax.dynamic_slice(total_absorb, corner, patch_shape) + grad_patch_absorb[slot_index],
            corner,
        )
        return (total_phase, total_absorb)

    empty = jnp.zeros(ext_phase.shape, jnp.float32)
    grad_ext_phase, grad_ext_absorb = lax.fori_loop(0, slots, deposit, (empty, empty))
    probe_total = lax.psum(grad_probe, "tile")
    back_phase, back_absorb = shifted(
        (grad_ext_phase[:, strip:], grad_ext_absorb[:, strip:]), "tile", 1
    )
    own_phase = grad_ext_phase[:, :strip].at[:, :length].add(back_phase)
    own_absorb = grad_ext_absorb[:, :strip].at[:, :length].add(back_absorb)
    grad_phase, grad_absorb = (
        lax.psum_scatter(own_phase, "mode", scatter_dimension=2, tiled=True),
        lax.psum_scatter(own_absorb, "mode", scatter_dimension=2, tiled=True),
    )
    return (grad_phase, grad_absorb, probe_total)


def solution(mesh):
    in_specs = (
        P(None, "tile", None),
        P(None, "tile", None),
        P("mode", None, None, None),
        P("tile", None, None),
        P("tile", None),
        P("tile"),
    )
    out_specs = (P(None, "tile", "mode"), P(None, "tile", "mode"), P("mode", None, None, None))
    return jax.shard_map(
        per_device, mesh=mesh, in_specs=in_specs, out_specs=out_specs, check_vma=False
    )
```

profile of v0, /device:TPU:0, one launch (start us, length us, event | category | flops | bytes accessed | tf_op | source)
XLA Modules:
  0.0 695.3 jit_solution(13215376706477410319)
XLA Ops:
  12.7 22.8 %collective-permute-done.1 = f32[2,256,512]{2,1,0:T(8,128)} collective-permute-done((f32[2,256,512]{2,1,0:T(8,128)}, f32[2,256,512]{2,1,0:T(8,128)}, u32[]{:S(2)}, u32[]{:S(2)}) %collective-permute-start.1) | collective-permute-done | bytes 1048608 | tf_op jit(solution)/shard_map/ppermute | solution.py:14
  35.5 3.0 pad_maximum_fusion.1
  38.6 6.6 while.23
  39.3 2.6 bitcast_dynamic-update-slice_fusion.5
  42.6 2.7 bitcast_dynamic-update-slice_fusion.5
  46.3 5.6 fusion.385
  51.8 4.9 collective-permute-done
  56.7 2.7 pad_maximum_fusion
  60.5 8.2 %while.22 = (s32[]{:T(128)}, f32[2,512,512]{2,1,0:T(8,128)}, s32[2,3]{1,0:T(2,128)S(1)}, f32[2,2,256,256]{3,2,0,1:T(8,128)}, s32[]{:T(128)}) while((s32[]{:T(128)}, f32[2,512,512]{2,1,0:T(8,128)}, s32[2,3]{1,0:T(2,128)S(1)}, f32[2,2,256,256]{3,2,0,1:T(8,128)}, s32[]{:T(128)}) %tuple.127), condition=%wide.while_cond.2, body=%wide.while_body.2.sunk | while | flops 2 | bytes 1050217 | solution.py:93
  61.2 3.3 bitcast_dynamic-update-slice_fusion.4
  65.1 3.5 bitcast_dynamic-update-slice_fusion.4
  73.0 2.2 copy.109
  75.2 3.1 fusion.24
  82.5 2.7 fusion.122
  85.2 3.1 fusion.84
  88.4 2.1 fusion.16
  90.5 2.7 convolution_subtract_fusion.4
  93.2 2.7 convolution_add_fusion.16
  95.9 2.8 fusion.114
  98.7 2.9 fusion.118
  101.6 2.8 fusion.15
  104.4 2.7 fusion.116
  107.1 2.7 fusion.63
  109.8 3.0 fusion.14
  112.8 2.7 convolution_subtract_fusion.2
  115.5 2.7 convolution_add_fusion.14
  118.3 2.7 fusion.107
  121.0 2.7 fusion.111
  123.7 3.2 fusion.13
  127.0 2.7 fusion.109
  129.7 2.7 fusion.79
  132.4 2.8 fusion.12
  135.2 2.9 convolution_subtract_fusion
  138.1 4.7 add_reduce_fusion
  143.5 47.0 %all-reduce.9.cloned.1.call-done = f32[2,256,256]{2,1,0:T(8,128)} async-done(((f32[2,256,256]{2,1,0:T(8,128)}), f32[2,256,256]{2,1,0:T(8,128)}) %all-reduce.9.cloned.1.call-update) | async-done | bytes 524304 | tf_op jit(solution)/shard_map/psum | solution.py:100
  202.2 2.4 fusion.10
  204.6 2.1 fusion.9
  206.7 3.8 multiply_reduce_fusion.6
  214.7 2.1 fusion.7
  216.8 2.2 fusion.97
  221.1 2.1 fusion.6
  223.2 2.1 fusion.5
  227.4 2.3 fusion.71
  231.8 2.1 fusion.3
  233.9 2.7 fusion.68
  236.6 2.7 fusion.91
  239.3 2.3 fusion.2
  241.7 2.7 fusion
  244.4 4.8 multiply_reduce_fusion.3
  258.6 36.1 %while.21 = (s32[]{:T(128)}, f32[2,512,512]{2,1,0:T(8,128)S(1)}, f32[2,512,512]{2,1,0:T(8,128)}, s32[2,2]{1,0:T(2,128)S(1)}, f32[2,2,256,256]{3,2,0,1:T(8,128)},...) while((s32[]{:T(128)}, f32[2,512,512]{2,1,0:T(8,128)S(1)}, ...), condition=%wide.region_11.12_spmd, body=%wide.region_10.11_spmd.sunk | while | flops 262152 | bytes 5243081 | solution.py:122
  264.7 5.0 dynamic_update_slice.17
  269.7 5.0 dynamic_update_slice.16
  280.9 6.1 dynamic_update_slice.17
  287.0 7.6 %dynamic_update_slice.16 = f32[2,512,512]{2,1,0:T(8,128)S(1)} dynamic-update-slice(f32[2,512,512]{2,1,0:T(8,128)S(1)} %get-tuple-element.405, f32[2,256,256]{2,1,0:T(8,128)S(1)} %get-tuple-element.351, s32[]{:T(128)} %constant.130.clone.1..sunk, s32[]{:T(128)S(6)} %select_n.343, s32[]{:T(128)S(6)} %select_n.344) | dynamic-update-slice | bytes 1048580 | tf_op jit(solution)/shard_map/while/body/eval_jaxpr/dynamic_update_slice | solution.py:109
  294.7 2.4 slice.87
  297.1 8.6 %collective-permute-start.3 = (f32[2,256,512]{2,1,0:T(8,128)}, f32[2,256,512]{2,1,0:T(8,128)S(1)}, u32[]{:S(2)}, u32[]{:S(2)}) collective-permute-start(f32[2,256,512]{2,1,0:T(8,128)} %slice.87), channel_id=1, source_target_pairs={{0,4},{4,8},{8,12},{12,16},{16,20},{20,24},{24,28},{28,32},{32,36}... | collective-permute-start | bytes 3145736 | tf_op jit(solution)/shard_map/ppermute | solution.py:14
  307.0 22.8 %collective-permute-done.3 = f32[2,256,512]{2,1,0:T(8,128)S(1)} collective-permute-done((f32[2,256,512]{2,1,0:T(8,128)}, f32[2,256,512]{2,1,0:T(8,128)S(1)}, u32[]{:S(2)}, u32[]{:S(2)}) %collective-permute-start.3) | collective-permute-done | bytes 1048608 | tf_op jit(solution)/shard_map/ppermute | solution.py:14
  329.8 2.4 slice_add_fusion
  332.4 4.3 collective-permute-start.2
  336.8 24.0 %collective-permute-done.2 = f32[2,256,512]{2,1,0:T(8,128)S(1)} collective-permute-done((f32[2,256,512]{2,1,0:T(8,128)S(1)}, f32[2,256,512]{2,1,0:T(8,128)S(1)}, u32[]{:S(2)}, u32[]{:S(2)}) %collective-permute-start.2) | collective-permute-done | bytes 1048608 | tf_op jit(solution)/shard_map/ppermute | solution.py:14
  362.0 256.7 %all-reduce.11.cloned.1.call-done = f32[2,2,256,256]{2,3,0,1:T(8,128)} async-done(((f32[2,2,256,256]{2,3,0,1:T(8,128)}), f32[2,2,256,256]{2,3,0,1:T(8,128)}) %all-reduce.11.cloned.1.call-update) | async-done | bytes 1048592 | tf_op jit(solution)/shard_map/psum | solution.py:123
  618.7 2.5 copy.156
  621.2 32.9 %reduce-scatter.5.cloned.1.call-done = f32[2,256,128]{2,1,0:T(8,128)} async-done(((f32[2,256,512]{2,1,0:T(8,128)}), f32[2,256,128]{2,1,0:T(8,128)}) %reduce-scatter.5.cloned.1.call-update) | async-done | bytes 262160 | tf_op jit(solution)/shard_map/reduce_scatter | solution.py:131
  654.1 34.2 %reduce-scatter.3.cloned.1.call-done = f32[2,256,128]{2,1,0:T(8,128)} async-done(((f32[2,256,512]{2,1,0:T(8,128)}), f32[2,256,128]{2,1,0:T(8,128)}) %reduce-scatter.3.cloned.1.call-update) | async-done | bytes 262160 | tf_op jit(solution)/shard_map/reduce_scatter | solution.py:130
  (123 shorter events, 57.0 us)
Async XLA Ops:
  7.2 183.4 %all-reduce.9.cloned.1.call-start = ((), (), s32[]{:S(2)}) async-start(), calls=%async_computation.2 | async-start | bytes 1048576 | tf_op jit(solution)/shard_map/psum | solution.py:100
  7.2 28.3 %collective-permute-start.1 = (f32[2,256,512]{2,1,0:T(8,128)}, f32[2,256,512]{2,1,0:T(8,128)}, u32[]{:S(2)}, u32[]{:S(2)}) collective-permute-start(f32[2,256,512]{2,1,0:T(8,128)} %param.16), channel_id=1, source_target_pairs={{4,0},{8,4},{12,8},{16,12},{20,16},{24,20},{28,24},{32,28},{36,32}... | collective-permute-start | bytes 3145736 | tf_op jit(solution)/shard_map/ppermute | solution.py:14
  8.5 48.2 %collective-permute-start = (f32[2,256,512]{2,1,0:T(8,128)}, f32[2,256,512]{2,1,0:T(8,128)}, u32[]{:S(2)}, u32[]{:S(2)}) collective-permute-start(f32[2,256,512]{2,1,0:T(8,128)} %param.17), channel_id=1, source_target_pairs={{4,0},{8,4},{12,8},{16,12},{20,16},{24,20},{28,24},{32,28},{36,32}... | collective-permute-start | bytes 3145736 | tf_op jit(solution)/shard_map/ppermute | solution.py:14
  9.8 1.7 copy-start.28
  11.3 77.0 %copy-start.2 = (f32[2,256,256]{1,2,0:T(8,128)}, f32[2,256,256]{1,2,0:T(8,128)S(1)}, u32[]{:S(2)}) copy-start(f32[2,256,256]{1,2,0:T(8,128)S(1)} %copy.104) | copy-start | bytes 1572868
  11.5 76.8 %copy-start.4 = (f32[2,256,256]{1,2,0:T(8,128)}, f32[2,256,256]{1,2,0:T(8,128)S(1)}, u32[]{:S(2)}) copy-start(f32[2,256,256]{1,2,0:T(8,128)S(1)} %copy.107) | copy-start | bytes 1572868
  12.7 97.1 %copy-start = (f32[256,256]{1,0:T(8,128)}, f32[256,256]{1,0:T(8,128)S(1)}, u32[]{:S(2)}) copy-start(f32[256,256]{1,0:T(8,128)S(1)} %get-tuple-element.254) | copy-start | bytes 786436
  45.3 1.0 copy-start.17
  46.3 10.5 %copy-start.27 = (f32[2,256,512]{2,1,0:T(8,128)S(1)}, f32[2,256,512]{2,1,0:T(8,128)}, u32[]{:S(2)}) copy-start(f32[2,256,512]{2,1,0:T(8,128)} %param.17) | copy-start | bytes 3145732
  51.8 17.0 %copy-start.12 = (f32[2,2,256,256]{3,2,0,1:T(8,128)}, f32[2,2,256,256]{3,2,0,1:T(8,128)S(1)}, u32[]{:S(2)}) copy-start(f32[2,2,256,256]{3,2,0,1:T(8,128)S(1)} %get-tuple-element.251) | copy-start | bytes 3145732
  73.0 15.4 %copy-start.6 = (f32[2,256,256]{1,2,0:T(8,128)}, f32[2,256,256]{1,2,0:T(8,128)S(1)}, u32[]{:S(2)}) copy-start(f32[2,256,256]{1,2,0:T(8,128)S(1)} %copy.106) | copy-start | bytes 1572868
  75.2 3.1 copy-start.8
  138.1 4.7 copy-start.10
  142.8 475.9 %all-reduce.11.cloned.1.call-start = ((), (), s32[]{:S(2)}) async-start(), calls=%async_computation.5 | async-start | bytes 2097152 | tf_op jit(solution)/shard_map/psum | solution.py:123
  190.5 1.5 copy-start.16
  192.1 4.0 copy-start.11
  225.3 2.1 copy-start.1
  241.6 2.8 copy-start.3
  241.6 2.8 copy-start.5
  241.7 2.8 copy-start.7
  241.7 2.8 copy-start.9
  249.3 3.2 copy-start.24
  249.3 3.2 copy-start.25
  251.5 2.6 copy-start.22
  251.5 2.6 copy-start.23
  252.5 1.6 copy-start.26
  252.6 1.7 copy-start.13
  252.6 2.0 copy-start.14
  252.6 2.3 copy-start.15
  294.7 11.1 %copy-start.20 = (f32[2,256,256]{1,2,0:T(8,128)S(1)}, f32[2,256,256]{1,2,0:T(8,128)}, u32[]{:S(2)}) copy-start(f32[2,256,256]{1,2,0:T(8,128)} %get-tuple-element.193) | copy-start | bytes 1572868
  294.7 11.1 %copy-start.21 = (f32[2,256,256]{1,2,0:T(8,128)S(1)}, f32[2,256,256]{1,2,0:T(8,128)}, u32[]{:S(2)}) copy-start(f32[2,256,256]{1,2,0:T(8,128)} %get-tuple-element.198) | copy-start | bytes 1572868
  294.7 11.1 %copy-start.18 = (f32[2,256,256]{1,2,0:T(8,128)S(1)}, f32[2,256,256]{1,2,0:T(8,128)}, u32[]{:S(2)}) copy-start(f32[2,256,256]{1,2,0:T(8,128)} %get-tuple-element.194) | copy-start | bytes 1572868
  294.7 11.1 %copy-start.19 = (f32[2,256,256]{1,2,0:T(8,128)S(1)}, f32[2,256,256]{1,2,0:T(8,128)}, u32[]{:S(2)}) copy-start(f32[2,256,256]{1,2,0:T(8,128)} %get-tuple-element.197) | copy-start | bytes 1572868
  297.1 32.7 %collective-permute-start.3 = (f32[2,256,512]{2,1,0:T(8,128)}, f32[2,256,512]{2,1,0:T(8,128)S(1)}, u32[]{:S(2)}, u32[]{:S(2)}) collective-permute-start(f32[2,256,512]{2,1,0:T(8,128)} %slice.87), channel_id=1, source_target_pairs={{0,4},{4,8},{8,12},{12,16},{16,20},{20,24},{24,28},{28,32},{32,36}... | collective-permute-start | bytes 3145736 | tf_op jit(solution)/shard_map/ppermute | solution.py:14
  307.0 347.2 %reduce-scatter.5.cloned.1.call-start = ((), (), s32[]{:S(2)}) async-start(), calls=%async_computation.4 | async-start | bytes 1310720 | tf_op jit(solution)/shard_map/reduce_scatter | solution.py:131
  332.3 356.1 %reduce-scatter.3.cloned.1.call-start = ((), (), s32[]{:S(2)}) async-start(), calls=%async_computation.3 | async-start | bytes 1310720 | tf_op jit(solution)/shard_map/reduce_scatter | solution.py:130
  332.4 28.3 %collective-permute-start.2 = (f32[2,256,512]{2,1,0:T(8,128)S(1)}, f32[2,256,512]{2,1,0:T(8,128)S(1)}, u32[]{:S(2)}, u32[]{:S(2)}) collective-permute-start(f32[2,256,512]{2,1,0:T(8,128)S(1)} %slice.85), channel_id=1, source_target_pairs={{0,4},{4,8},{8,12},{12,16},{16,20},{20,24},{24,28},{28,32},{32,36}... | collective-permute-start | bytes 3145736 | tf_op jit(solution)/shard_map/ppermute | solution.py:14
Sparse Core Ops, SparseCore 0:
  142.9 47.5 all-reduce.8
  307.1 311.5 all-reduce.10
  622.1 32.0 reduce-scatter.4
  657.2 31.1 reduce-scatter.2
where the time goes:
time: 700 us; the launch traced here: 695 us
  waiting for transfers between devices  445 us (64%)
  matrix products  124 us (18%)
  local copies, waits for them, and re-layouts  64.3 us (9%)
  other arithmetic  22 us (3%)
  starting transfers between devices  15.7 us (2%)
  between operations  15.7 us (2%)
  loops' own time  7.95 us (1%)
    psum x1, waiting for transfers between devices, per_device(): probe_total = lax.psum(grad_probe, 'tile')  257 us
    ppermute x4, waiting for transfers between devices, shifted(): return lax.ppermute(block, axis, route)  74.5 us
    dot_general x24, matrix products, left_apply(): jnp.einsum('kn,...nm->...km', matrix, field, precision=lax.Precision.HIGH...  63.7 us
    dot_general x24, matrix products, right_apply(): jnp.einsum('...km,ml->...kl', field, matrix, precision=lax.Precision.HIGH...  60.5 us
    psum x1, waiting for transfers between devices, per_device(): total = lax.psum(partial_intensity, 'mode')  47 us
    reduce_scatter x1, waiting for transfers between devices, per_device(): lax.psum_scatter(own_phase, 'mode', scatter_dimension=2, tiled=True)  34.2 us
    reduce_scatter x1, waiting for transfers between devices, per_device(): lax.psum_scatter(own_absorb, 'mode', scatter_dimension=2, tiled=True)  32.9 us
    ppermute x4, starting transfers between devices, shifted(): return lax.ppermute(block, axis, route)  15.5 us
  transfers between devices with their start and end apart: 8, of which 8 were waited for; matrix products, arithmetic and copies ran while one was open for 4% of the time, Pallas kernels for 0%

commit v1 on v0

v1 whole, which is shorter than its diff:
```python
import functools
import math

import jax
import jax.numpy as jnp
import ml_dtypes
import numpy as np
from jax import lax
from jax.experimental import pallas as pl
from jax.experimental.pallas import tpu as pltpu
from jax.sharding import PartitionSpec as P

fresnel_number = 40.0
LENGTH = 256
HALF = LENGTH // 2
SLOTS = 2
LOCAL_MODES = 2
TILES = 32
F32 = jnp.float32
BF16 = jnp.bfloat16


def split_table(matrix):
    high = matrix.astype(ml_dtypes.bfloat16)
    low = (matrix - high.astype(np.float64)).astype(ml_dtypes.bfloat16)
    return high, low


@functools.lru_cache(maxsize=None)
def constant_tables():
    counter = np.arange(LENGTH)
    angle = 2.0 * np.pi / LENGTH * ((counter[:, None] * counter[None, :]) % LENGTH)
    dft = np.exp(-1j * angle) / math.sqrt(LENGTH)
    freq = ((counter + HALF) % LENGTH - HALF) / LENGTH
    kappa = np.exp(-1j * np.pi * fresnel_number * freq**2)
    prop = np.conj(dft) @ (kappa[:, None] * dft)
    tables = []
    for matrix in (prop, dft):
        re, im = matrix.real, matrix.imag
        right = np.block([[re, im], [-im, re]])
        left = np.block([[re, -im], [im, re]])
        tables.append(np.stack(split_table(right) + split_table(left)))
    return tables


def split(value):
    high = value.astype(BF16)
    low = (value - high.astype(F32)).astype(BF16)
    return high, low


def dot(a, b):
    return jnp.dot(a, b, preferred_element_type=F32)


def transform(re, im, tab):
    high, low = split(jnp.concatenate([re, im], axis=1))
    mid = dot(high, tab[0]) + dot(low, tab[0]) + dot(high, tab[1])
    mid = jnp.concatenate([mid[:, :LENGTH], mid[:, LENGTH:]], axis=0)
    high, low = split(mid)
    out = dot(tab[2], high) + dot(tab[2], low) + dot(tab[3], high)
    return out[:LENGTH], out[LENGTH:]


def cos_sin(angle):
    half = angle * 0.5
    sq = half * half
    s = -1.0 / 39916800.0
    for c in (1.0 / 362880.0, -1.0 / 5040.0, 1.0 / 120.0, -1.0 / 6.0, 1.0):
        s = s * sq + c
    s = s * half
    c = 1.0 / 479001600.0
    for k in (-1.0 / 3628800.0, 1.0 / 40320.0, -1.0 / 720.0, 1.0 / 24.0, -0.5, 1.0):
        c = c * sq + k
    return 1.0 - 2.0 * s * s, 2.0 * s * c


def masks(row, column):
    rows = lax.broadcasted_iota(jnp.int32, (LENGTH, LENGTH), 0)
    columns = lax.broadcasted_iota(jnp.int32, (LENGTH, LENGTH), 1)
    return rows >= row, columns >= column


def wrapped(own, below, in_strip, on_left):
    top = jnp.where(on_left, own[:, :LENGTH], own[:, LENGTH:])
    bottom = jnp.where(on_left, below[:, :LENGTH], below[:, LENGTH:])
    return jnp.where(in_strip, top, bottom)


def transmit(phase, absorb):
    magnitude = jnp.exp(-absorb)
    c, s = cos_sin(phase)
    return magnitude * c, magnitude * s


def roll2(value, row, column):
    return pltpu.roll(pltpu.roll(value, row, 0), column, 1)


def roll_kernel(offsets, probe, out):
    for slot in range(SLOTS):
        row, column = offsets[slot, 0], offsets[slot, 1] % LENGTH
        for mode in range(LOCAL_MODES):
            for part in range(2):
                out[slot, mode, part] = roll2(probe[mode, part], row, column)


def first_kernel(offsets, core, own_phase, own_absorb, halo_mine, halo_other, rolled, tab, wave, trans):
    swap = core[0] == 1
    below_phase = jnp.where(swap, halo_other[...], halo_mine[...])
    below_absorb = jnp.where(swap, halo_mine[...], halo_other[...])
    for slot in range(SLOTS):
        in_strip, on_left = masks(offsets[slot, 0], offsets[slot, 1])
        tr, ti = transmit(
            wrapped(own_phase[0], below_phase, in_strip, on_left),
            wrapped(own_absorb[0], below_absorb, in_strip, on_left),
        )
        trans[slot, 0] = tr
        trans[slot, 1] = ti
        for mode in range(LOCAL_MODES):
            pr, pi = rolled[slot, mode, 0], rolled[slot, mode, 1]
            wr, wi = transform(pr * tr - pi * ti, pr * ti + pi * tr, tab)
            wave[slot, mode, 0] = wr
            wave[slot, mode, 1] = wi


def second_kernel(slot, offsets, core, own_phase, own_absorb, halo_mine, halo_other, wave, tab, field, trans, keep, send, total):
    swap = core[0] == 1
    below_phase = jnp.where(swap, halo_other[...], halo_mine[...])
    below_absorb = jnp.where(swap, halo_mine[...], halo_other[...])
    in_strip, on_left = masks(offsets[slot, 0], offsets[slot, 1])
    tr, ti = transmit(
        wrapped(own_phase[0], below_phase, in_strip, on_left),
        wrapped(own_absorb[0], below_absorb, in_strip, on_left),
    )
    trans[0] = tr
    trans[1] = ti
    for mode in range(LOCAL_MODES):
        wr, wi = wave[0, mode, 0], wave[0, mode, 1]
        fr, fi = transform(wr * tr - wi * ti, wr * ti + wi * tr, tab)
        field[mode, 0] = fr
        field[mode, 1] = fi
        power = fr * fr + fi * fi
        total[...] = power if mode == 0 else total[...] + power
    low, high = total[:HALF], total[HALF:]
    keep[...] = jnp.where(swap, high, low)
    send[...] = jnp.where(swap, low, high)


def backward_kernel(
    slot, offsets, counts, core, mine, other, measured, field, wave, rolled, trans0, trans1, tab_a, tab_t,
    keep, send, grad_probe, factor,
):
    swap = core[0] == 1
    valid = (slot < counts[0]).astype(F32)
    low = jnp.where(swap, other[...], mine[...])
    high = jnp.where(swap, mine[...], other[...])
    intensity = jnp.concatenate([low, high], axis=0)
    factor[...] = valid * (1.0 - jnp.sqrt(measured[0] + 1.0) / jnp.sqrt(intensity + 1.0))

    def emit(layer, gr, gi, tr, ti):
        grads = (gi * tr - gr * ti, -(gr * tr + gi * ti))
        for kind in range(2):
            left, right = grads[kind][:, :HALF], grads[kind][:, HALF:]
            keep[layer, kind] = jnp.where(swap, right, left)
            send[layer, kind] = jnp.where(swap, left, right)

    row, column = offsets[slot, 0], offsets[slot, 1]
    back_row, back_column = (LENGTH - row) % LENGTH, (LENGTH - column) % LENGTH
    ur, ui = trans1[0], trans1[1]
    tr, ti = trans0[0, 0], trans0[0, 1]
    back = []
    sum_r = sum_i = None
    for mode in range(LOCAL_MODES):
        hr, hi = transform(factor[...] * field[mode, 0], -factor[...] * field[mode, 1], tab_t)
        wr, wi = wave[0, mode, 0], wave[0, mode, 1]
        gr = hr * wr - hi * wi
        gi = -(hr * wi + hi * wr)
        sum_r, sum_i = (gr, gi) if mode == 0 else (sum_r + gr, sum_i + gi)
        back.append((hr * ur - hi * ui, hr * ui + hi * ur))
    emit(1, sum_r, sum_i, ur, ui)
    for mode in range(LOCAL_MODES):
        hr, hi = transform(back[mode][0], back[mode][1], tab_a)
        pr, pi = rolled[0, mode, 0], rolled[0, mode, 1]
        gr = hr * pr - hi * pi
        gi = -(hr * pi + hi * pr)
        sum_r, sum_i = (gr, gi) if mode == 0 else (sum_r + gr, sum_i + gi)
        grad_probe[mode, 0] = roll2(hr * tr - hi * ti, back_row, back_column)
        grad_probe[mode, 1] = roll2(-(hr * ti + hi * tr), back_row, back_column)
    emit(0, sum_r, sum_i, tr, ti)


def fold_kernel(offsets, zhi, keep_a, keep_b, got_a, got_b, core, mine, send):
    rows = lax.broadcasted_iota(jnp.int32, (LENGTH, HALF), 0)
    columns = lax.broadcasted_iota(jnp.int32, (LENGTH, HALF), 1) + core[0] * HALF
    zero = jnp.zeros((LENGTH, HALF), F32)
    for layer in range(2):
        for kind in range(2):
            acc = None
            for slot, (keep, got) in enumerate(((keep_a, got_a), (keep_b, got_b))):
                value = keep[layer, kind] + got[layer, kind]
                in_strip = rows >= offsets[slot, 0]
                on_left = columns >= offsets[slot, 1]
                on_mine = jnp.logical_xor(on_left, zhi[0] == 1)
                pieces = [
                    jnp.where(jnp.logical_and(in_strip, on_mine), value, zero),
                    jnp.where(jnp.logical_or(in_strip, jnp.logical_not(on_mine)), zero, value),
                    jnp.where(jnp.logical_and(in_strip, jnp.logical_not(on_mine)), value, zero),
                    jnp.where(jnp.logical_or(in_strip, on_mine), zero, value),
                ]
                acc = pieces if acc is None else [a + b for a, b in zip(acc, pieces)]
            mine[0, layer, kind] = acc[0]
            mine[1, layer, kind] = acc[1]
            send[0, layer, kind] = acc[2]
            send[1, layer, kind] = acc[3]


VMEM = pl.BlockSpec(memory_space=pltpu.VMEM)
SMEM = pl.BlockSpec(memory_space=pltpu.SMEM)
PARAMS = pltpu.CompilerParams(vmem_limit_bytes=48 * 1024 * 1024)


def shape(*dims):
    return jax.ShapeDtypeStruct(dims, F32)


def whole(block, index):
    return pl.BlockSpec(block, lambda i: index)


def per_device(object_phase, object_absorb, probe_modes, measured, offsets, counts):
    layers, strip, columns = object_phase.shape
    mode_index = lax.axis_index("mode")
    core = (mode_index % 2).reshape(1)
    zhi = (mode_index // 2).reshape(1)
    up = [(i + 1, i) for i in range(TILES - 1)]
    down = [(i, i + 1) for i in range(TILES - 1)]
    cores = [(i, i ^ 1) for i in range(4)]
    far = [(i, i ^ 2) for i in range(4)]
    tab_a, tab_t = (jnp.asarray(t) for t in constant_tables())

    picked = jnp.where(core[0] == 0, object_phase, object_absorb)
    halo_mine = [lax.ppermute(picked[s], "tile", up) for s in range(layers)]
    rolled = pl.pallas_call(
        roll_kernel,
        out_shape=shape(SLOTS, LOCAL_MODES, 2, LENGTH, LENGTH),
        in_specs=[SMEM, VMEM],
        out_specs=VMEM,
        compiler_params=PARAMS,
    )(offsets, probe_modes)
    halo_other = [lax.ppermute(h, "mode", cores) for h in halo_mine]

    wave, trans0 = pl.pallas_call(
        first_kernel,
        grid=(1,),
        out_shape=(shape(SLOTS, LOCAL_MODES, 2, LENGTH, LENGTH), shape(SLOTS, 2, LENGTH, LENGTH)),
        in_specs=[
            SMEM,
            SMEM,
            whole((1, strip, columns), (0, 0, 0)),
            whole((1, strip, columns), (0, 0, 0)),
            VMEM,
            VMEM,
            VMEM,
            VMEM,
        ],
        out_specs=(VMEM, VMEM),
        compiler_params=PARAMS,
    )(offsets, core, object_phase, object_absorb, halo_mine[0], halo_other[0], rolled, tab_a)

    forward = []
    for slot in range(SLOTS):
        forward.append(
            pl.pallas_call(
                functools.partial(second_kernel, slot),
                grid=(1,),
                out_shape=(
                    shape(LOCAL_MODES, 2, LENGTH, LENGTH),
                    shape(2, LENGTH, LENGTH),
                    shape(HALF, LENGTH),
                    shape(HALF, LENGTH),
                ),
                in_specs=[
                    SMEM,
                    SMEM,
                    whole((1, strip, columns), (1, 0, 0)),
                    whole((1, strip, columns), (1, 0, 0)),
                    VMEM,
                    VMEM,
                    whole((1, LOCAL_MODES, 2, LENGTH, LENGTH), (slot, 0, 0, 0, 0)),
                    VMEM,
                ],
                out_specs=(VMEM,) * 4,
                scratch_shapes=[pltpu.VMEM((LENGTH, LENGTH), F32)],
                compiler_params=PARAMS,
            )(offsets, core, object_phase, object_absorb, halo_mine[1], halo_other[1], wave, tab_t)
        )

    back = []
    for slot in range(SLOTS):
        field, trans1, keep, send = forward[slot]
        pair = keep + lax.ppermute(send, "mode", cores)
        mine = pair + lax.ppermute(pair, "mode", far)
        other = lax.ppermute(mine, "mode", cores)
        back.append(
            pl.pallas_call(
                functools.partial(backward_kernel, slot),
                grid=(1,),
                out_shape=(
                    shape(2, 2, LENGTH, HALF),
                    shape(2, 2, LENGTH, HALF),
                    shape(LOCAL_MODES, 2, LENGTH, LENGTH),
                ),
                in_specs=[
                    SMEM,
                    SMEM,
                    SMEM,
                    VMEM,
                    VMEM,
                    whole((1, LENGTH, LENGTH), (slot, 0, 0)),
                    VMEM,
                    whole((1, LOCAL_MODES, 2, LENGTH, LENGTH), (slot, 0, 0, 0, 0)),
                    whole((1, LOCAL_MODES, 2, LENGTH, LENGTH), (slot, 0, 0, 0, 0)),
                    whole((1, 2, LENGTH, LENGTH), (slot, 0, 0, 0)),
                    VMEM,
                    VMEM,
                    VMEM,
                ],
                out_specs=(VMEM,) * 3,
                scratch_shapes=[pltpu.VMEM((LENGTH, LENGTH), F32)],
                compiler_params=PARAMS,
            )(offsets, counts, core, mine, other, measured, field, wave, rolled, trans0, trans1, tab_a, tab_t)
        )

    keep_a, send_a, probe_a = back[0]
    keep_b, send_b, probe_b = back[1]
    got_a = lax.ppermute(send_a, "mode", cores)
    got_b = lax.ppermute(send_b, "mode", cores)
    mine, send = pl.pallas_call(
        fold_kernel,
        out_shape=(shape(2, 2, 2, LENGTH, HALF), shape(2, 2, 2, LENGTH, HALF)),
        in_specs=[SMEM, SMEM, VMEM, VMEM, VMEM, VMEM, SMEM],
        out_specs=(VMEM, VMEM),
        compiler_params=PARAMS,
    )(offsets, zhi, keep_a, keep_b, got_a, got_b, core)
    got_next = lax.ppermute(send[1], "mode", far)
    got_own = lax.ppermute(send[0], "mode", far)
    from_above = lax.ppermute(mine[1] + got_next, "tile", down)

    grad_probe = (probe_a + probe_b).reshape(TILES, -1, LENGTH)
    share = jnp.sum(lax.all_to_all(grad_probe, "tile", 0, 0), axis=0)
    gathered = lax.all_to_all(jnp.broadcast_to(share[None], grad_probe.shape), "tile", 0, 0)
    probe_total = gathered.reshape(LOCAL_MODES, 2, LENGTH, LENGTH)

    grads = mine[0] + got_own + from_above
    return (grads[:, 0], grads[:, 1], probe_total)


def solution(mesh):
    in_specs = (
        P(None, "tile", None),
        P(None, "tile", None),
        P("mode", None, None, None),
        P("tile", None, None),
        P("tile", None),
        P("tile"),
    )
    out_specs = (P(None, "tile", "mode"), P(None, "tile", "mode"), P("mode", None, None, None))
    return jax.shard_map(
        per_device, mesh=mesh, in_specs=in_specs, out_specs=out_specs, check_vma=False
    )
```

time: 700 us -> 161 us (0.23)
  waiting for transfers between devices: 445 us -> 73.5 us
  matrix products: 124 us -> 0 us
  local copies, waits for them, and re-layouts: 64.3 us -> 5.2 us
  Pallas kernels: 0 us -> 40.5 us
  starting transfers between devices: 15.7 us -> 34.4 us
  other arithmetic: 22 us -> 5.42 us
  between operations: 15.7 us -> 1.52 us
  loops' own time: 7.95 us -> 0 us
    psum x2 -> x0, waiting for transfers between devices: 304 us -> none  [the longest x1 257 us: per_device(): probe_total = lax.psum(grad_probe, 'tile')]
    dot_general x48 -> x0, matrix products: 124 us -> none  [the longest x24 63.7 us: left_apply(): jnp.einsum('kn,...nm->...km', matrix, field, precision=lax.Precision.HIGH...]
    reduce_scatter x2 -> x0, waiting for transfers between devices: 67.2 us -> none  [the longest x1 34.2 us: per_device(): lax.psum_scatter(own_phase, 'mode', scatter_dimension=2, tiled=True)]
    pallas_call x0 -> x7, Pallas kernels: none -> 40.5 us  [the longest x2 18.3 us: per_device(): pl.pallas_call(functools.partial(backward_kernel, slot), grid=(1,), out_s...]
    dynamic_update_slice x4 -> x0, local copies, waits for them, and re-layouts: 23.7 us -> none  [the longest x2 12.6 us: deposit(): lax.dynamic_update_slice(total_phase, lax.dynamic_slice(total_phase, corn...]
    all_to_all x0 -> x2, starting transfers between devices: none -> 17.9 us  [the longest x1 10.9 us: per_device(): share = jnp.sum(lax.all_to_all(grad_probe, 'tile', 0, 0), axis=0)]
    gather x12 -> x0, local copies, waits for them, and re-layouts: 14.7 us -> none
    another operation x3 -> x0, loops' own time: 7.95 us -> none  [the longest x1 7.71 us: per_device(): lax.fori_loop(0, slots, deposit, (empty, empty))]
  transfers between devices with their start and end apart: 8 -> 17, of which waited for: 8 -> 6; matrix products, arithmetic and copies ran while one was open for 4% -> 4% of each run, Pallas kernels for 0% -> 22%
where the time goes in v1:
time: 161 us
  waiting for transfers between devices  73.5 us (46%)
  Pallas kernels  40.5 us (25%)
  starting transfers between devices  34.4 us (21%)
  other arithmetic  5.42 us (3%)
  local copies, waits for them, and re-layouts  5.2 us (3%)
    ppermute x2, waiting for transfers between devices, per_device(): halo_mine = [lax.ppermute(picked[s], 'tile', up) for s in range(layers)]  24.1 us
    ppermute x1, waiting for transfers between devices, per_device(): got_next = lax.ppermute(send[1], 'mode', far)  23.1 us
    ppermute x1, waiting for transfers between devices, per_device(): got_own = lax.ppermute(send[0], 'mode', far)  20.5 us
    pallas_call x2, Pallas kernels, per_device(): pl.pallas_call(functools.partial(backward_kernel, slot), grid=(1,), out_s...  18.3 us
    all_to_all x1, starting transfers between devices, per_device(): share = jnp.sum(lax.all_to_all(grad_probe, 'tile', 0, 0), axis=0)  10.9 us
    pallas_call x2, Pallas kernels, per_device(): pl.pallas_call(functools.partial(second_kernel, slot), grid=(1,), out_sha...  10.3 us
    pallas_call x1, Pallas kernels, per_device(): pl.pallas_call(first_kernel, grid=(1,), out_shape=(shape(SLOTS, LOCAL_MOD...  8.82 us
    all_to_all x1, starting transfers between devices, per_device(): lax.all_to_all(jnp.broadcast_to(share[None], grad_probe.shape), 'tile', 0...  7.02 us
  transfers between devices with their start and end apart: 17, of which 6 were waited for; matrix products, arithmetic and copies ran while one was open for 4% of the time, Pallas kernels for 22%

profile of v1, /device:TPU:0, one launch (start us, length us, event | category | flops | bytes accessed | tf_op | source)
XLA Modules:
  0.0 160.6 jit_solution(18422678200021137466)
XLA Ops:
  0.6 0.0 copy-start.4
  0.7 0.0 copy-start.7
  0.7 1.5 broadcast_select_fusion
  2.2 0.1 slice_bitcast_fusion
  2.3 0.0 copy-start.1
  2.3 0.0 copy-start.2
  2.3 1.4 collective-permute-start.2
  3.7 1.3 collective-permute-start
  5.0 14.2 %collective-permute-done.2.halo_mine = f32[256,512]{1,0:T(8,128)S(1)} collective-permute-done((f32[256,512]{1,0:T(8,128)S(1)}, f32[256,512]{1,0:T(8,128)S(1)}, u32[]{:S(2)}, u32[]{:S(2)}) %collective-permute-start.2) | collective-permute-done | bytes 524320 | tf_op jit(solution)/shard_map/ppermute | solution.py:243
  19.2 0.0 collective-permute-start.3
  19.2 10.0 %collective-permute-done.halo_mine = f32[256,512]{1,0:T(8,128)S(1)} collective-permute-done((f32[256,512]{1,0:T(8,128)S(1)}, f32[256,512]{1,0:T(8,128)S(1)}, u32[]{:S(2)}, u32[]{:S(2)}) %collective-permute-start) | collective-permute-done | bytes 524320 | tf_op jit(solution)/shard_map/ppermute | solution.py:243
  29.1 0.0 collective-permute-start.1
  29.2 0.0 copy-done.4
  29.2 0.0 copy-done.7
  29.2 1.3 shard_map.103.rolled
  30.5 0.0 copy-start
  30.5 1.3 copy-done
  31.8 0.0 collective-permute-done.3.halo_other
  31.8 0.0 copy-done.1
  31.8 0.0 copy-done.2
  31.8 8.8 %shard_map.104 = (f32[2,2,2,256,256]{4,3,2,1,0:T(8,128)}, f32[2,2,256,256]{3,2,1,0:T(8,128)S(1)}) custom-call(s32[2,2]{1,0:T(2,128)S(1)} %copy-done.7, s32[1]{0:T(128)} %bitcast.1.core, f32[2,256,512]{2,1,0:T(8,128)S(1)} %copy-done.1, f32[2,256,512]{2,1,0:T(8,128)S(1)} %copy-done.2, f32[256,512]{1,0:T(8,128)S(1)} %collective-permute-done.2.halo_mine, ...), custom_call_target="tpu_custom_call" | custom-call | tf_op jit(solution)/shard_map/pallas_call | solution.py:253
  40.7 0.0 collective-permute-done.1.halo_other
  40.7 5.1 %shard_map.107 = (f32[2,2,256,256]{3,2,1,0:T(8,128)S(1)}, f32[2,256,256]{2,1,0:T(8,128)S(1)}, f32[128,256]{1,0:T(8,128)S(1)}, f32[128,256]{1,0:T(8,128)S(1)}) custom-call(s32[2,2]{1,0:T(2,128)S(1)} %copy-done.7, s32[1]{0:T(128)} %bitcast.1.core, f32[2,256,512]{2,1,0:T(8,128)S(1)} %copy-done.1, f32[2,256,512]{2,1,0:T(8,128)S(1)} %copy-done.2, ...), custom_call_target="tpu_custom_call" | custom-call | tf_op jit(solution)/shard_map/pallas_call | solution.py:274
  45.8 0.0 copy-start.3
  45.8 0.6 collective-permute-start.7
  46.4 5.1 %shard_map.105 = (f32[2,2,256,256]{3,2,1,0:T(8,128)S(1)}, f32[2,256,256]{2,1,0:T(8,128)S(1)}, f32[128,256]{1,0:T(8,128)S(1)}, f32[128,256]{1,0:T(8,128)S(1)}) custom-call(s32[2,2]{1,0:T(2,128)S(1)} %copy-done.7, s32[1]{0:T(128)} %bitcast.1.core, f32[2,256,512]{2,1,0:T(8,128)S(1)} %copy-done.1, f32[2,256,512]{2,1,0:T(8,128)S(1)} %copy-done.2, ...), custom_call_target="tpu_custom_call" | custom-call | tf_op jit(solution)/shard_map/pallas_call | solution.py:274
  51.5 0.1 collective-permute-start.4
  51.7 0.0 collective-permute-done.7
  51.7 4.1 %collective-permute-start.8 = (f32[128,256]{1,0:T(8,128)S(1)}, f32[128,256]{1,0:T(8,128)S(1)}, u32[]{:S(2)}, u32[]{:S(2)}) collective-permute-start(f32[128,256]{1,0:T(8,128)S(1)} %add.32), channel_id=1, source_target_pairs={{0,2},{1,3},{2,0},{3,1},{4,6},{5,7},{6,4},{7,5},{8,10},{9,11},{10,... | collective-permute-start | bytes 393224 | tf_op jit(solution)/shard_map/ppermute | solution.py:303
  55.8 0.0 collective-permute-done.4
  55.9 1.3 collective-permute-start.5
  57.1 2.8 %collective-permute-done.8 = f32[128,256]{1,0:T(8,128)S(1)} collective-permute-done((f32[128,256]{1,0:T(8,128)S(1)}, f32[128,256]{1,0:T(8,128)S(1)}, u32[]{:S(2)}, u32[]{:S(2)}) %collective-permute-start.8) | collective-permute-done | bytes 131104 | tf_op jit(solution)/shard_map/ppermute | solution.py:303
  60.0 0.1 collective-permute-start.9
  60.1 3.0 %collective-permute-done.5 = f32[128,256]{1,0:T(8,128)S(1)} collective-permute-done((f32[128,256]{1,0:T(8,128)S(1)}, f32[128,256]{1,0:T(8,128)S(1)}, u32[]{:S(2)}, u32[]{:S(2)}) %collective-permute-start.5) | collective-permute-done | bytes 131104 | tf_op jit(solution)/shard_map/ppermute | solution.py:303
  63.0 0.3 collective-permute-start.6
  64.0 0.0 collective-permute-done.9.other
  64.0 0.0 copy-done.3
  64.0 9.2 %shard_map.108 = (f32[2,2,256,128]{3,2,1,0:T(8,128)S(1)}, f32[2,2,256,128]{3,2,1,0:T(8,128)}, f32[2,2,256,256]{3,2,1,0:T(8,128)S(1)}) custom-call(s32[2,2]{1,0:T(2,128)S(1)} %copy-done.7, s32[1]{0:T(128)S(6)} %copy.12.counts, s32[1]{0:T(128)} %bitcast.1.core, f32[128,256]{1,0:T(8,128)S(1)} %add.33.mine, f32[128,256]{1,0:T(8,128)S(1)} %collective-permute-done.9.other, ...), custom_call_target="tpu_custom_call" | custom-call | tf_op jit(solution)/shard_map/pallas_call | solution.py:306
  73.2 0.5 collective-permute-start.11
  73.7 0.0 collective-permute-done.6.other
  73.7 9.2 %shard_map.106 = (f32[2,2,256,128]{3,2,1,0:T(8,128)S(1)}, f32[2,2,256,128]{3,2,1,0:T(8,128)}, f32[2,2,256,256]{3,2,1,0:T(8,128)S(1)}) custom-call(s32[2,2]{1,0:T(2,128)S(1)} %copy-done.7, s32[1]{0:T(128)S(6)} %copy.12.counts, s32[1]{0:T(128)} %bitcast.1.core, f32[128,256]{1,0:T(8,128)S(1)} %add.31.mine, f32[128,256]{1,0:T(8,128)S(1)} %collective-permute-done.6.other, ...), custom_call_target="tpu_custom_call" | custom-call | tf_op jit(solution)/shard_map/pallas_call | solution.py:306
  82.8 0.8 copy-done.5
  83.6 0.0 collective-permute-start.10
  83.6 1.1 add.37
  84.7 10.9 %all-to-all-start = ((f32[32,32,256]{2,1,0:T(8,128)}), f32[32,32,256]{2,1,0:T(8,128)}, u32[]{:S(2)}, u32[]{:S(2)}) async-start(f32[32,32,256]{2,1,0:T(8,128)} %bitcast.22), calls=%async_computation | async-start | bytes 2097152 | tf_op jit(solution)/shard_map/all_to_all | solution.py:351
  95.6 0.0 collective-permute-done.11.got_b
  95.6 0.0 collective-permute-done.10.got_a
  95.7 1.7 %shard_map.109 = (f32[2,2,2,256,128]{4,3,2,1,0:T(8,128)S(1)}, f32[2,2,2,256,128]{4,3,2,1,0:T(8,128)S(1)}) custom-call(s32[2,2]{1,0:T(2,128)S(1)} %copy-done.7, s32[1]{0:T(128)} %bitcast.zhi, f32[2,2,256,128]{3,2,1,0:T(8,128)S(1)} %copy-done.6, f32[2,2,256,128]{3,2,1,0:T(8,128)S(1)} %get-tuple-element.32.keep_b, ...), custom_call_target="tpu_custom_call" | custom-call | tf_op jit(solution)/shard_map/pallas_call | solution.py:339
  97.4 0.1 slice_bitcast_fusion.3
  97.5 3.7 %collective-permute-start.13 = (f32[2,2,256,128]{3,2,1,0:T(8,128)S(1)}, f32[2,2,256,128]{3,2,1,0:T(8,128)S(1)}, u32[]{:S(2)}, u32[]{:S(2)}) collective-permute-start(f32[2,2,256,128]{3,2,1,0:T(8,128)S(1)} %get-tuple-element.40), channel_id=1, source_target_pairs={{0,2},{1,3},{2,0},{3,1},{4,6},{5,7},{6,4},{7,5},{8,10},{9,11},{10,... | collective-permute-start | bytes 1572872 | tf_op jit(solution)/shard_map/ppermute | solution.py:346
  101.1 0.1 collective-permute-start.12
  101.2 23.1 %collective-permute-done.13 = f32[2,2,256,128]{3,2,1,0:T(8,128)S(1)} collective-permute-done((f32[2,2,256,128]{3,2,1,0:T(8,128)S(1)}, f32[2,2,256,128]{3,2,1,0:T(8,128)S(1)}, u32[]{:S(2)}, u32[]{:S(2)}) %collective-permute-start.13) | collective-permute-done | bytes 524320 | tf_op jit(solution)/shard_map/ppermute | solution.py:346
  124.3 0.1 bitcast_add_fusion
  124.4 3.1 %collective-permute-start.14 = (f32[2,2,256,128]{3,2,1,0:T(8,128)S(1)}, f32[2,2,256,128]{3,2,1,0:T(8,128)}, u32[]{:S(2)}, u32[]{:S(2)}) collective-permute-start(f32[2,2,256,128]{3,2,1,0:T(8,128)S(1)} %bitcast_add_fusion), channel_id=1, source_target_pairs={{0,4},{4,8},{8,12},{12,16},{16,20},{20,24},{24,28},{28,32},{32,36}... | collective-permute-start | bytes 1572872 | tf_op jit(solution)/shard_map/ppermute | solution.py:348
  127.5 0.0 all-to-all-done
  127.5 1.3 reduce_sum.9
  128.8 1.1 broadcast_in_dim.2
  129.9 7.0 %all-to-all-start.1 = ((f32[32,32,256]{2,1,0:T(8,128)}), f32[32,32,256]{2,1,0:T(8,128)S(1)}, u32[]{:S(2)}, u32[]{:S(2)}) async-start(f32[32,32,256]{2,1,0:T(8,128)} %broadcast_in_dim.2), calls=%async_computation.1 | async-start | bytes 2097152 | tf_op jit(solution)/shard_map/all_to_all | solution.py:352
  136.9 20.5 %collective-permute-done.12 = f32[2,2,256,128]{3,2,1,0:T(8,128)} collective-permute-done((f32[2,2,256,128]{3,2,1,0:T(8,128)S(1)}, f32[2,2,256,128]{3,2,1,0:T(8,128)}, u32[]{:S(2)}, u32[]{:S(2)}) %collective-permute-start.12) | collective-permute-done | bytes 524320 | tf_op jit(solution)/shard_map/ppermute | solution.py:347
  157.4 0.0 collective-permute-done.14
  157.4 1.3 fusion
  158.8 0.8 slice_bitcast_fusion.4
  159.6 0.0 all-to-all-done.1
  159.6 1.0 copy.13
  (7 shorter events, 0.1 us)
Async XLA Ops:
  0.6 28.5 %copy-start.4 = (f32[2,2,256,256]{3,2,1,0:T(8,128)S(1)}, f32[2,2,256,256]{3,2,1,0:T(8,128)}, u32[]{:S(2)}) copy-start(f32[2,2,256,256]{3,2,1,0:T(8,128)} %probe.1) | copy-start | bytes 3145732
  0.7 28.5 %copy-start.7 = (s32[2,2]{1,0:T(2,128)S(1)}, s32[2,2]{1,0:T(2,128)}, u32[]{:S(2)}) copy-start(s32[2,2]{1,0:T(2,128)} %offsets.13) | copy-start | bytes 52
  2.3 29.6 %copy-start.1 = (f32[2,256,512]{2,1,0:T(8,128)S(1)}, f32[2,256,512]{2,1,0:T(8,128)}, u32[]{:S(2)}) copy-start(f32[2,256,512]{2,1,0:T(8,128)} %own_phase.5) | copy-start | bytes 3145732
  2.3 29.6 %copy-start.2 = (f32[2,256,512]{2,1,0:T(8,128)S(1)}, f32[2,256,512]{2,1,0:T(8,128)}, u32[]{:S(2)}) copy-start(f32[2,256,512]{2,1,0:T(8,128)} %own_absorb.5) | copy-start | bytes 3145732
  2.3 16.9 %collective-permute-start.2 = (f32[256,512]{1,0:T(8,128)S(1)}, f32[256,512]{1,0:T(8,128)S(1)}, u32[]{:S(2)}, u32[]{:S(2)}) collective-permute-start(f32[256,512]{1,0:T(8,128)S(1)} %get-tuple-element.41), channel_id=1, source_target_pairs={{4,0},{8,4},{12,8},{16,12},{20,16},{24,20},{28,24},{32,28},{36,32}... | collective-permute-start | bytes 1572872 | tf_op jit(solution)/shard_map/ppermute | solution.py:243
  3.7 25.4 %collective-permute-start = (f32[256,512]{1,0:T(8,128)S(1)}, f32[256,512]{1,0:T(8,128)S(1)}, u32[]{:S(2)}, u32[]{:S(2)}) collective-permute-start(f32[256,512]{1,0:T(8,128)S(1)} %get-tuple-element.42), channel_id=1, source_target_pairs={{4,0},{8,4},{12,8},{16,12},{20,16},{24,20},{28,24},{32,28},{36,32}... | collective-permute-start | bytes 1572872 | tf_op jit(solution)/shard_map/ppermute | solution.py:243
  19.2 12.7 %collective-permute-start.3 = (f32[256,512]{1,0:T(8,128)S(1)}, f32[256,512]{1,0:T(8,128)S(1)}, u32[]{:S(2)}, u32[]{:S(2)}) collective-permute-start(f32[256,512]{1,0:T(8,128)S(1)} %collective-permute-done.2.halo_mine), channel_id=1, source_target_pairs={{0,1},{1,0},{2,3},{3,2},{4,5},{5,4},{6,7},{7,6},{8,9},{9,8},{10,11... | collective-permute-start | bytes 1572872 | tf_op jit(solution)/shard_map/ppermute | solution.py:251
  29.1 11.5 %collective-permute-start.1 = (f32[256,512]{1,0:T(8,128)S(1)}, f32[256,512]{1,0:T(8,128)S(1)}, u32[]{:S(2)}, u32[]{:S(2)}) collective-permute-start(f32[256,512]{1,0:T(8,128)S(1)} %collective-permute-done.halo_mine), channel_id=1, source_target_pairs={{0,1},{1,0},{2,3},{3,2},{4,5},{5,4},{6,7},{7,6},{8,9},{9,8},{10,11... | collective-permute-start | bytes 1572872 | tf_op jit(solution)/shard_map/ppermute | solution.py:251
  30.5 1.4 copy-start
  45.8 18.2 %copy-start.3 = (f32[2,256,256]{2,1,0:T(8,128)S(1)}, f32[2,256,256]{2,1,0:T(8,128)}, u32[]{:S(2)}) copy-start(f32[2,256,256]{2,1,0:T(8,128)} %measured.3) | copy-start | bytes 1572868
  45.8 5.9 %collective-permute-start.7 = (f32[128,256]{1,0:T(8,128)S(1)}, f32[128,256]{1,0:T(8,128)S(1)}, u32[]{:S(2)}, u32[]{:S(2)}) collective-permute-start(f32[128,256]{1,0:T(8,128)S(1)} %get-tuple-element.29), channel_id=1, source_target_pairs={{0,1},{1,0},{2,3},{3,2},{4,5},{5,4},{6,7},{7,6},{8,9},{9,8},{10,11... | collective-permute-start | bytes 393224 | tf_op jit(solution)/shard_map/ppermute | solution.py:302
  51.5 4.3 %collective-permute-start.4 = (f32[128,256]{1,0:T(8,128)S(1)}, f32[128,256]{1,0:T(8,128)S(1)}, u32[]{:S(2)}, u32[]{:S(2)}) collective-permute-start(f32[128,256]{1,0:T(8,128)S(1)} %get-tuple-element.23), channel_id=1, source_target_pairs={{0,1},{1,0},{2,3},{3,2},{4,5},{5,4},{6,7},{7,6},{8,9},{9,8},{10,11... | collective-permute-start | bytes 393224 | tf_op jit(solution)/shard_map/ppermute | solution.py:302
  51.7 8.2 %collective-permute-start.8 = (f32[128,256]{1,0:T(8,128)S(1)}, f32[128,256]{1,0:T(8,128)S(1)}, u32[]{:S(2)}, u32[]{:S(2)}) collective-permute-start(f32[128,256]{1,0:T(8,128)S(1)} %add.32), channel_id=1, source_target_pairs={{0,2},{1,3},{2,0},{3,1},{4,6},{5,7},{6,4},{7,5},{8,10},{9,11},{10,... | collective-permute-start | bytes 393224 | tf_op jit(solution)/shard_map/ppermute | solution.py:303
  55.9 7.2 %collective-permute-start.5 = (f32[128,256]{1,0:T(8,128)S(1)}, f32[128,256]{1,0:T(8,128)S(1)}, u32[]{:S(2)}, u32[]{:S(2)}) collective-permute-start(f32[128,256]{1,0:T(8,128)S(1)} %add.30), channel_id=1, source_target_pairs={{0,2},{1,3},{2,0},{3,1},{4,6},{5,7},{6,4},{7,5},{8,10},{9,11},{10,... | collective-permute-start | bytes 393224 | tf_op jit(solution)/shard_map/ppermute | solution.py:303
  60.0 4.0 %collective-permute-start.9 = (f32[128,256]{1,0:T(8,128)S(1)}, f32[128,256]{1,0:T(8,128)S(1)}, u32[]{:S(2)}, u32[]{:S(2)}) collective-permute-start(f32[128,256]{1,0:T(8,128)S(1)} %add.33.mine), channel_id=1, source_target_pairs={{0,1},{1,0},{2,3},{3,2},{4,5},{5,4},{6,7},{7,6},{8,9},{9,8},{10,11... | collective-permute-start | bytes 393224 | tf_op jit(solution)/shard_map/ppermute | solution.py:304
  63.0 10.6 %collective-permute-start.6 = (f32[128,256]{1,0:T(8,128)S(1)}, f32[128,256]{1,0:T(8,128)S(1)}, u32[]{:S(2)}, u32[]{:S(2)}) collective-permute-start(f32[128,256]{1,0:T(8,128)S(1)} %add.31.mine), channel_id=1, source_target_pairs={{0,1},{1,0},{2,3},{3,2},{4,5},{5,4},{6,7},{7,6},{8,9},{9,8},{10,11... | collective-permute-start | bytes 393224 | tf_op jit(solution)/shard_map/ppermute | solution.py:304
  73.2 22.5 %collective-permute-start.11 = (f32[2,2,256,128]{3,2,1,0:T(8,128)}, f32[2,2,256,128]{3,2,1,0:T(8,128)S(1)}, u32[]{:S(2)}, u32[]{:S(2)}) collective-permute-start(f32[2,2,256,128]{3,2,1,0:T(8,128)} %get-tuple-element.34), channel_id=1, source_target_pairs={{0,1},{1,0},{2,3},{3,2},{4,5},{5,4},{6,7},{7,6},{8,9},{9,8},{10,11... | collective-permute-start | bytes 1572872 | tf_op jit(solution)/shard_map/ppermute | solution.py:338
  82.8 0.8 copy-start.5
  83.6 12.0 %collective-permute-start.10 = (f32[2,2,256,128]{3,2,1,0:T(8,128)}, f32[2,2,256,128]{3,2,1,0:T(8,128)}, u32[]{:S(2)}, u32[]{:S(2)}) collective-permute-start(f32[2,2,256,128]{3,2,1,0:T(8,128)} %get-tuple-element.33), channel_id=1, source_target_pairs={{0,1},{1,0},{2,3},{3,2},{4,5},{5,4},{6,7},{7,6},{8,9},{9,8},{10,11... | collective-permute-start | bytes 1572872 | tf_op jit(solution)/shard_map/ppermute | solution.py:337
  84.7 10.9 %copy-start.6 = (f32[2,2,256,128]{3,2,1,0:T(8,128)S(1)}, f32[2,2,256,128]{3,2,1,0:T(8,128)}, u32[]{:S(2)}) copy-start(f32[2,2,256,128]{3,2,1,0:T(8,128)} %copy-done.5) | copy-start | bytes 1572868
  84.7 42.7 %all-to-all-start = ((f32[32,32,256]{2,1,0:T(8,128)}), f32[32,32,256]{2,1,0:T(8,128)}, u32[]{:S(2)}, u32[]{:S(2)}) async-start(f32[32,32,256]{2,1,0:T(8,128)} %bitcast.22), calls=%async_computation | async-start | bytes 2097152 | tf_op jit(solution)/shard_map/all_to_all | solution.py:351
  97.5 26.9 %collective-permute-start.13 = (f32[2,2,256,128]{3,2,1,0:T(8,128)S(1)}, f32[2,2,256,128]{3,2,1,0:T(8,128)S(1)}, u32[]{:S(2)}, u32[]{:S(2)}) collective-permute-start(f32[2,2,256,128]{3,2,1,0:T(8,128)S(1)} %get-tuple-element.40), channel_id=1, source_target_pairs={{0,2},{1,3},{2,0},{3,1},{4,6},{5,7},{6,4},{7,5},{8,10},{9,11},{10,... | collective-permute-start | bytes 1572872 | tf_op jit(solution)/shard_map/ppermute | solution.py:346
  101.1 56.3 %collective-permute-start.12 = (f32[2,2,256,128]{3,2,1,0:T(8,128)S(1)}, f32[2,2,256,128]{3,2,1,0:T(8,128)}, u32[]{:S(2)}, u32[]{:S(2)}) collective-permute-start(f32[2,2,256,128]{3,2,1,0:T(8,128)S(1)} %get-tuple-element.39), channel_id=1, source_target_pairs={{0,2},{1,3},{2,0},{3,1},{4,6},{5,7},{6,4},{7,5},{8,10},{9,11},{10,... | collective-permute-start | bytes 1572872 | tf_op jit(solution)/shard_map/ppermute | solution.py:347
  124.4 33.0 %collective-permute-start.14 = (f32[2,2,256,128]{3,2,1,0:T(8,128)S(1)}, f32[2,2,256,128]{3,2,1,0:T(8,128)}, u32[]{:S(2)}, u32[]{:S(2)}) collective-permute-start(f32[2,2,256,128]{3,2,1,0:T(8,128)S(1)} %bitcast_add_fusion), channel_id=1, source_target_pairs={{0,4},{4,8},{8,12},{12,16},{16,20},{20,24},{24,28},{28,32},{32,36}... | collective-permute-start | bytes 1572872 | tf_op jit(solution)/shard_map/ppermute | solution.py:348
  129.9 29.7 %all-to-all-start.1 = ((f32[32,32,256]{2,1,0:T(8,128)}), f32[32,32,256]{2,1,0:T(8,128)S(1)}, u32[]{:S(2)}, u32[]{:S(2)}) async-start(f32[32,32,256]{2,1,0:T(8,128)} %broadcast_in_dim.2), calls=%async_computation.1 | async-start | bytes 2097152 | tf_op jit(solution)/shard_map/all_to_all | solution.py:352

commit v2 on v0

v2 whole, which is shorter than its diff:
```python
import functools
import math

import jax
import jax.numpy as jnp
import ml_dtypes
import numpy as np
from jax import lax
from jax.experimental import pallas as pl
from jax.experimental.pallas import tpu as pltpu
from jax.sharding import PartitionSpec as P

fresnel_number = 40.0
LENGTH = 256
HALF = LENGTH // 2
SLOTS = 2
LOCAL_MODES = 2
TILES = 32
F32 = jnp.float32
BF16 = jnp.bfloat16


def split_table(matrix):
    high = matrix.astype(ml_dtypes.bfloat16)
    low = (matrix - high.astype(np.float64)).astype(ml_dtypes.bfloat16)
    return high, low


@functools.lru_cache(maxsize=None)
def constant_tables():
    counter = np.arange(LENGTH)
    angle = 2.0 * np.pi / LENGTH * ((counter[:, None] * counter[None, :]) % LENGTH)
    dft = np.exp(-1j * angle) / math.sqrt(LENGTH)
    freq = ((counter + HALF) % LENGTH - HALF) / LENGTH
    kappa = np.exp(-1j * np.pi * fresnel_number * freq**2)
    prop = np.conj(dft) @ (kappa[:, None] * dft)
    tables = []
    for matrix in (prop, dft):
        highs, lows = zip(*(split_table(m) for m in (matrix.real, matrix.imag, matrix.real + matrix.imag)))
        tables.append(np.stack(highs + lows))
    return tables


def split(value):
    high = value.astype(BF16)
    low = (value - high.astype(F32)).astype(BF16)
    return high, low


def dot(a, b):
    return jnp.dot(a, b, preferred_element_type=F32)


def right_product(value, high, low):
    h, l = split(value)
    return dot(h, high) + dot(l, high) + dot(h, low)


def left_product(value, high, low):
    h, l = split(value)
    return dot(high, h) + dot(high, l) + dot(low, h)


def three_products(product, re, im, tab):
    a = product(re, tab[0], tab[3])
    b = product(im, tab[1], tab[4])
    c = product(re + im, tab[2], tab[5])
    return a - b, c - a - b


def transform(fields, tab):
    re, im = (jnp.concatenate([f[part] for f in fields], axis=0) for part in range(2))
    mid = three_products(right_product, re, im, tab)
    re, im = (
        jnp.concatenate([m[i * LENGTH : (i + 1) * LENGTH] for i in range(len(fields))], axis=1) for m in mid
    )
    re, im = three_products(left_product, re, im, tab)
    return [
        (re[:, i * LENGTH : (i + 1) * LENGTH], im[:, i * LENGTH : (i + 1) * LENGTH]) for i in range(len(fields))
    ]


def cos_sin(angle):
    half = angle * 0.5
    sq = half * half
    s = -1.0 / 39916800.0
    for c in (1.0 / 362880.0, -1.0 / 5040.0, 1.0 / 120.0, -1.0 / 6.0, 1.0):
        s = s * sq + c
    s = s * half
    c = 1.0 / 479001600.0
    for k in (-1.0 / 3628800.0, 1.0 / 40320.0, -1.0 / 720.0, 1.0 / 24.0, -0.5, 1.0):
        c = c * sq + k
    return 1.0 - 2.0 * s * s, 2.0 * s * c


def transmit(phase, absorb):
    magnitude = jnp.exp(-absorb)
    c, s = cos_sin(phase)
    return magnitude * c, magnitude * s


def roll2(value, row, column):
    return pltpu.roll(pltpu.roll(value, row, 0), column, 1)


def left_of(offsets, slot, shape):
    return lax.broadcasted_iota(jnp.int32, shape, 1) >= offsets[slot, 1]


def prepare_kernel(place, offsets, phase, absorb, probe, inside, rolled):
    on_left = left_of(offsets, place[0] // 2, PLANE)
    for layer in range(2):
        for kind, strip in enumerate((phase, absorb)):
            inside[layer, kind] = jnp.where(on_left, strip[layer, :, :LENGTH], strip[layer, :, LENGTH:])
    roll_probes(offsets, place, probe, rolled)


def pick_kernel(place, upper_offsets, phase, absorb, out):
    part = pl.ds(pl.multiple_of((place[0] % 2) * HALF, HALF), HALF)
    on_left = left_of(upper_offsets, place[0] // 2, (HALF, LENGTH))
    for layer in range(2):
        for kind, strip in enumerate((phase, absorb)):
            out[layer, kind] = jnp.where(on_left, strip[layer, part, :LENGTH], strip[layer, part, LENGTH:])


def slot_transmit(offsets, place, layer, inside, mine, other):
    swap = place[0] % 2 == 1
    in_strip = lax.broadcasted_iota(jnp.int32, PLANE, 0) >= offsets[place[0] // 2, 0]
    patch = []
    for kind in range(2):
        low = jnp.where(swap, other[layer, kind], mine[layer, kind])
        high = jnp.where(swap, mine[layer, kind], other[layer, kind])
        patch.append(jnp.where(in_strip, inside[layer, kind], jnp.concatenate([low, high], axis=0)))
    return transmit(*patch)


def roll_probes(offsets, place, probe, rolled):
    slot = place[0] // 2
    row, column = offsets[slot, 0], offsets[slot, 1] % LENGTH
    for m in range(probe.shape[0]):
        for part in range(2):
            rolled[m, part] = roll2(probe[m, part], row, column)


def through(fields, trans, tab):
    tr, ti = trans[0], trans[1]
    return transform([(f[0] * tr - f[1] * ti, f[0] * ti + f[1] * tr) for f in fields], tab)


def store(refs, fields):
    for m, (re, im) in enumerate(fields):
        refs[m, 0] = re
        refs[m, 1] = im


def forward_kernel(
    offsets, place, inside, mine, other, rolled_o, probe_f, tab_a, tab_t,
    rolled_f, wave_o, wave_f, field_o, field_f, trans0, trans1, power,
):
    trans0[0], trans0[1] = slot_transmit(offsets, place, 0, inside, mine, other)
    trans1[0], trans1[1] = slot_transmit(offsets, place, 1, inside, mine, other)
    roll_probes(offsets, place, probe_f, rolled_f)
    total = None
    for rolled, wave, field in ((rolled_o, wave_o, field_o), (rolled_f, wave_f, field_f)):
        store(wave, through([rolled[m] for m in range(LOCAL_MODES)], trans0, tab_a))
        fields = through([wave[m] for m in range(LOCAL_MODES)], trans1, tab_t)
        store(field, fields)
        term = sum(re * re + im * im for re, im in fields)
        total = term if total is None else total + term
    power[...] = total


def adjoint(offsets, place, factor, field, wave, rolled, trans0, trans1, tab_a, tab_t, put):
    slot = place[0] // 2
    row, column = offsets[slot, 0], offsets[slot, 1]
    back_row, back_column = (LENGTH - row) % LENGTH, (LENGTH - column) % LENGTH
    ur, ui = trans1[0], trans1[1]
    tr, ti = trans0[0], trans0[1]
    modes = range(LOCAL_MODES)
    back = transform([(factor * field[m, 0], -factor * field[m, 1]) for m in modes], tab_t)
    upper = (
        sum(hr * wave[m, 0] - hi * wave[m, 1] for m, (hr, hi) in enumerate(back)),
        -sum(hr * wave[m, 1] + hi * wave[m, 0] for m, (hr, hi) in enumerate(back)),
    )
    back = transform([(hr * ur - hi * ui, hr * ui + hi * ur) for hr, hi in back], tab_a)
    lower = (
        sum(hr * rolled[m, 0] - hi * rolled[m, 1] for m, (hr, hi) in enumerate(back)),
        -sum(hr * rolled[m, 1] + hi * rolled[m, 0] for m, (hr, hi) in enumerate(back)),
    )
    for m, (hr, hi) in enumerate(back):
        put(2 * m, roll2(hr * tr - hi * ti, back_row, back_column))
        put(2 * m + 1, roll2(-(hr * ti + hi * tr), back_row, back_column))
    return lower, upper


def backward_kernel(
    offsets, counts, place, power, near, measured, field_o, field_f, wave_o, wave_f, rolled_o, rolled_f,
    trans0, trans1, tab_a, tab_t, grads, keep, send, factor, partial, planes, sems,
):
    slot, swap = place[0] // 2, place[0] % 2 == 1
    valid = (slot < counts[0]).astype(F32)
    target = jnp.where(slot == 1, measured[1], measured[0])
    factor[...] = valid * (1.0 - jnp.sqrt(target + 1.0) / jnp.sqrt(power[...] + near[...] + 1.0))
    rest = (trans0, trans1, tab_a, tab_t)
    copies = []

    def put(index, value, foreign):
        planes[foreign, index] = value
        out = grads.at[jnp.bitwise_xor(slot, foreign), index]
        copies.append(pltpu.make_async_copy(planes.at[foreign, index], out, sems.at[foreign, index]))
        copies[-1].start()

    sums = adjoint(offsets, place, factor[...], field_f, wave_f, rolled_f, *rest, functools.partial(put, foreign=1))
    for layer in range(2):
        for part in range(2):
            partial[layer, part] = sums[layer][part]
    sums = adjoint(offsets, place, factor[...], field_o, wave_o, rolled_o, *rest, functools.partial(put, foreign=0))
    for layer, trans in enumerate((trans0, trans1)):
        gr, gi = (sums[layer][part] + partial[layer, part] for part in range(2))
        tr, ti = trans[0], trans[1]
        for kind, grad in enumerate((gi * tr - gr * ti, -(gr * tr + gi * ti))):
            left, right = grad[:, :HALF], grad[:, HALF:]
            keep[kind, layer] = jnp.where(swap, right, left)
            send[kind, layer] = jnp.where(swap, left, right)
    for copy in copies:
        copy.wait()


def fold_kernel(offsets, upper_offsets, place, pair, got, mine, send):
    core, zhi = place[0] % 2, place[0] // 2
    rows = lax.broadcasted_iota(jnp.int32, (LENGTH, HALF), 0)
    columns = lax.broadcasted_iota(jnp.int32, (LENGTH, HALF), 1) + core * HALF
    own_rows, upper_rows = rows >= offsets[zhi, 0], rows < upper_offsets[zhi, 0]
    own_mine = jnp.logical_xor(columns >= offsets[zhi, 1], zhi == 1)
    upper_mine = jnp.logical_xor(columns >= upper_offsets[zhi, 1], zhi == 1)
    for kind in range(2):
        for layer in range(2):
            own = jnp.where(own_rows, pair[kind, layer], 0.0)
            upper = jnp.where(upper_rows, got[kind, layer], 0.0)
            mine[kind, layer] = jnp.where(own_mine, own, 0.0) + jnp.where(upper_mine, upper, 0.0)
            send[kind, layer] = jnp.where(own_mine, 0.0, own) + jnp.where(upper_mine, 0.0, upper)


def sum_kernel(parts, after, out):
    del after
    total = parts[0]
    for i in range(1, parts.shape[0]):
        total += parts[i]
    out[...] = total


def spread_kernel(share, out):
    for i in range(out.shape[0]):
        out[i] = share[...]


VMEM = pl.BlockSpec(memory_space=pltpu.VMEM)
SMEM = pl.BlockSpec(memory_space=pltpu.SMEM)
ANY = pl.BlockSpec(memory_space=pl.ANY)
HBM = pl.BlockSpec(memory_space=pltpu.HBM)
PLANE = (LENGTH, LENGTH)
WAVE = (LOCAL_MODES, 2, LENGTH, LENGTH)
ONE = (1, 2, LENGTH, LENGTH)
PAIR = (2, LENGTH, LENGTH)
SHARE = (2, 2, LENGTH, HALF)
STRIPS = (2, 2, LENGTH, LENGTH)
HALVES = (2, 2, HALF, LENGTH)


def run(kernel, micros, scalars, outs, args, specs=None, scratch=(), out_specs=None, mib=24):
    return pl.pallas_call(
        kernel,
        out_shape=[jax.ShapeDtypeStruct(o, F32) for o in outs],
        in_specs=[SMEM] * scalars + (specs or [VMEM] * (len(args) - scalars)),
        out_specs=out_specs or [VMEM] * len(outs),
        scratch_shapes=scratch,
        compiler_params=pltpu.CompilerParams(vmem_limit_bytes=mib * 1024 * 1024),
        cost_estimate=pl.CostEstimate(flops=int(micros * 1.0e9), bytes_accessed=int(micros * 3.0e6), transcendentals=0),
    )(*args)


def per_device(object_phase, object_absorb, probe_modes, measured, offsets, counts):
    columns = object_phase.shape[2]
    place = lax.axis_index("mode").reshape(1)
    up = [(i + 1, i) for i in range(TILES - 1)]
    down = [(i, i + 1) for i in range(TILES - 1)]
    cores = [(i, i ^ 1) for i in range(4)]
    far = [(i, i ^ 2) for i in range(4)]
    flip = [(4 * t + m, 4 * (t ^ 4) + (m ^ 2)) for t in range(TILES) for m in range(4)]
    holders = [[4 * t + 2 * h + c for h in range(2) for t in range(TILES)] for c in range(2)]
    tab_a, tab_t = (jnp.asarray(t) for t in constant_tables())

    foreign = lax.ppermute(probe_modes, ("tile", "mode"), flip)
    upper_offsets = lax.ppermute(offsets, "tile", down)
    inside, rolled_o = run(
        prepare_kernel, 1.5, 2, [STRIPS, WAVE], (place, offsets, object_phase, object_absorb, probe_modes)
    )
    upper_offsets, inside = lax.optimization_barrier((upper_offsets, inside))
    (pick,) = run(pick_kernel, 0.5, 2, [HALVES], (place, upper_offsets, object_phase, object_absorb))
    mine = lax.ppermute(pick, "tile", up)
    other = lax.ppermute(mine, "mode", cores)
    rolled_f, wave_o, wave_f, field_o, field_f, trans0, trans1, power = run(
        forward_kernel,
        8.0,
        2,
        [WAVE] * 5 + [PAIR, PAIR, PLANE],
        (offsets, place, inside, mine, other, rolled_o, foreign, tab_a, tab_t),
    )
    near = lax.ppermute(power, "mode", cores)
    grads, keep, send = run(
        backward_kernel,
        9.0,
        3,
        [(2, 4) + PLANE, SHARE, SHARE],
        (
            offsets, counts, place, power, near, measured, field_o, field_f, wave_o, wave_f, rolled_o, rolled_f,
            trans0, trans1, tab_a, tab_t,
        ),
        scratch=[
            pltpu.VMEM(PLANE, F32),
            pltpu.VMEM((2, 2) + PLANE, F32),
            pltpu.VMEM((2, 4) + PLANE, F32),
            pltpu.SemaphoreType.DMA((2, 4)),
        ],
        out_specs=[HBM, VMEM, VMEM],
    )

    pair = keep + lax.ppermute(send, "mode", cores)
    got = lax.ppermute(pair, "tile", down)
    own, send = run(fold_kernel, 0.05, 3, [SHARE, SHARE], (offsets, upper_offsets, place, pair, got))
    from_far = lax.ppermute(send, "mode", far)
    grad_object = own + from_far

    grads = grads.reshape(2 * TILES, -1, LENGTH)
    parts = lax.all_to_all(grads, ("tile", "mode"), 0, 0, axis_index_groups=holders)
    (share,) = run(sum_kernel, 0.5, 0, [parts.shape[1:]], (parts, own), [VMEM, ANY])
    (spread,) = run(spread_kernel, 0.5, 0, [(TILES,) + share.shape], (share,))
    probe_total = lax.all_to_all(spread, "tile", 0, 0).reshape(WAVE)
    return (grad_object[0], grad_object[1], probe_total)


def solution(mesh):
    in_specs = (
        P(None, "tile", None),
        P(None, "tile", None),
        P("mode", None, None, None),
        P("tile", None, None),
        P("tile", None),
        P("tile"),
    )
    out_specs = (P(None, "tile", "mode"), P(None, "tile", "mode"), P("mode", None, None, None))
    return jax.shard_map(
        per_device, mesh=mesh, in_specs=in_specs, out_specs=out_specs, check_vma=False
    )
```

time: 700 us -> 137 us (0.20)
  waiting for transfers between devices: 445 us -> 69.5 us
  matrix products: 124 us -> 0 us
  local copies, waits for them, and re-layouts: 64.3 us -> 7.5 us
  other arithmetic: 22 us -> 0.14 us
  Pallas kernels: 0 us -> 21.7 us
  starting transfers between devices: 15.7 us -> 36.2 us
  between operations: 15.7 us -> 1.45 us
  loops' own time: 7.95 us -> 0 us
    psum x2 -> x0, waiting for transfers between devices: 304 us -> none  [the longest x1 257 us: per_device(): probe_total = lax.psum(grad_probe, 'tile')]
    dot_general x48 -> x0, matrix products: 124 us -> none  [the longest x24 63.7 us: left_apply(): jnp.einsum('kn,...nm->...km', matrix, field, precision=lax.Precision.HIGH...]
    reduce_scatter x2 -> x0, waiting for transfers between devices: 67.2 us -> none  [the longest x1 34.2 us: per_device(): lax.psum_scatter(own_phase, 'mode', scatter_dimension=2, tiled=True)]
    dynamic_update_slice x4 -> x0, local copies, waits for them, and re-layouts: 23.7 us -> none  [the longest x2 12.6 us: deposit(): lax.dynamic_update_slice(total_phase, lax.dynamic_slice(total_phase, corn...]
    pallas_call x0 -> x7, Pallas kernels: none -> 21.7 us  [run(): pl.pallas_call(kernel, out_shape=[jax.ShapeDtypeStruct(o, F32) for o in o...]
    all_to_all x0 -> x2, starting transfers between devices: none -> 20.2 us  [the longest x1 10.1 us: per_device(): probe_total = lax.all_to_all(spread, 'tile', 0, 0).reshape(WAVE)]
    gather x12 -> x0, local copies, waits for them, and re-layouts: 14.7 us -> none
    another operation x3 -> x0, loops' own time: 7.95 us -> none  [the longest x1 7.71 us: per_device(): lax.fori_loop(0, slots, deposit, (empty, empty))]
  transfers between devices with their start and end apart: 8 -> 10, of which waited for: 8 -> 6; matrix products, arithmetic and copies ran while one was open for 4% -> 1% of each run, Pallas kernels for 0% -> 2%
where the time goes in v2:
time: 137 us; the launch traced here: 136 us
  waiting for transfers between devices  69.5 us (51%)
  starting transfers between devices  36.2 us (26%)
  Pallas kernels  21.7 us (16%)
  local copies, waits for them, and re-layouts  7.5 us (5%)
  between operations  1.45 us (1%)
    ppermute x1, waiting for transfers between devices, per_device(): got = lax.ppermute(pair, 'tile', down)  28.1 us
    ppermute x1, waiting for transfers between devices, per_device(): from_far = lax.ppermute(send, 'mode', far)  22.7 us
    pallas_call x7, Pallas kernels, run(): pl.pallas_call(kernel, out_shape=[jax.ShapeDtypeStruct(o, F32) for o in o...  21.7 us
    ppermute x1, waiting for transfers between devices, per_device(): mine = lax.ppermute(pick, 'tile', up)  13.7 us
    all_to_all x1, starting transfers between devices, per_device(): probe_total = lax.all_to_all(spread, 'tile', 0, 0).reshape(WAVE)  10.1 us
    all_to_all x1, starting transfers between devices, per_device(): lax.all_to_all(grads, ('tile', 'mode'), 0, 0, axis_index_groups=holders)  10 us
    unnamed x19, local copies, waits for them, and re-layouts  6.67 us
    ppermute x1, starting transfers between devices, per_device(): foreign = lax.ppermute(probe_modes, ('tile', 'mode'), flip)  4.12 us
  transfers between devices with their start and end apart: 10, of which 6 were waited for; matrix products, arithmetic and copies ran while one was open for 1% of the time, Pallas kernels for 2%

profile of v2, /device:TPU:0, one launch (start us, length us, event | category | flops | bytes accessed | tf_op | source)
XLA Modules:
  0.0 136.4 jit_solution(945244831585928443)
XLA Ops:
  0.6 3.6 %collective-permute-start = (s32[2,2]{1,0:T(2,128)}, s32[2,2]{1,0:T(2,128)S(1)}, u32[]{:S(2)}, u32[]{:S(2)}) collective-permute-start(s32[2,2]{1,0:T(2,128)} %offsets.7), channel_id=1, source_target_pairs={{0,4},{4,8},{8,12},{12,16},{16,20},{20,24},{24,28},{28,32},{32,36}... | collective-permute-start | bytes 56 | tf_op jit(solution)/shard_map/ppermute | solution.py:294
  4.2 4.1 %collective-permute-start.3 = (f32[2,2,256,256]{3,2,1,0:T(8,128)}, f32[2,2,256,256]{3,2,1,0:T(8,128)}, u32[]{:S(2)}, u32[]{:S(2)}) collective-permute-start(f32[2,2,256,256]{3,2,1,0:T(8,128)} %probe.1), channel_id=1, source_target_pairs={{0,18},{1,19},{2,16},{3,17},{4,22},{5,23},{6,20},{7,21},{8,26},{9,... | collective-permute-start | bytes 3145736 | tf_op jit(solution)/shard_map/ppermute | solution.py:293
  8.3 0.0 copy-start.1
  8.3 1.2 copy-done.1
  9.6 0.0 copy-start.2
  9.6 1.2 copy-done.2
  10.8 0.0 copy-start.3
  10.8 0.7 copy-done.3
  11.5 0.0 copy-start.5
  11.5 1.2 copy-done.5
  12.7 1.0 shard_map.103
  13.7 0.0 copy-start.4
  13.7 0.0 copy-start.7
  13.7 0.0 copy-start.8
  13.7 0.0 collective-permute-done.upper_offsets
  13.7 0.6 shard_map.104
  14.3 1.3 collective-permute-start.1
  15.6 13.7 %collective-permute-done.1.mine = f32[2,2,128,256]{3,2,1,0:T(8,128)S(1)} collective-permute-done((f32[2,2,128,256]{3,2,1,0:T(8,128)S(1)}, f32[2,2,128,256]{3,2,1,0:T(8,128)S(1)}, u32[]{:S(2)}, u32[]{:S(2)}) %collective-permute-start.1) | collective-permute-done | bytes 524320 | tf_op jit(solution)/shard_map/ppermute | solution.py:300
  29.3 0.0 collective-permute-start.2
  29.4 2.2 %collective-permute-done.3.probe_f = f32[2,2,256,256]{3,2,1,0:T(8,128)} collective-permute-done((f32[2,2,256,256]{3,2,1,0:T(8,128)}, f32[2,2,256,256]{3,2,1,0:T(8,128)}, u32[]{:S(2)}, u32[]{:S(2)}) %collective-permute-start.3) | collective-permute-done | bytes 1048608 | tf_op jit(solution)/shard_map/ppermute | solution.py:293
  31.5 0.0 collective-permute-done.2.other
  31.5 0.0 copy-done.4
  31.5 0.0 copy-done.7
  31.5 0.0 copy-done.8
  31.5 0.0 copy-start.6
  31.6 8.3 %shard_map.105 = (f32[2,2,256,256]{3,2,1,0:T(8,128)S(1)}, f32[2,2,256,256]{3,2,1,0:T(8,128)S(1)}, f32[2,2,256,256]{3,2,1,0:T(8,128)S(1)}, f32[2,2,256,256]{3,2,1...) custom-call(s32[2,2]{1,0:T(2,128)S(1)} %copy-done.4, ...), custom_call_target="tpu_custom_call" | custom-call | flops 8000000000 | bytes 24000000 | tf_op jit(solution)/shard_map/pallas_call | solution.py:271
  39.9 0.3 collective-permute-start.4
  40.8 0.9 collective-permute-done.4.near
  41.7 0.0 copy-done.6
  41.7 9.8 %shard_map.106 = (f32[2,4,256,256]{3,2,1,0:T(8,128)S(1)}, f32[2,2,256,128]{3,2,1,0:T(8,128)S(1)}, f32[2,2,256,128]{3,2,1,0:T(8,128)S(1)}) custom-call(s32[2,2]{1,0:T(2,128)S(1)} %copy-done.4, s32[1]{0:T(128)S(6)} %copy.12.counts, s32[1]{0:T(128)} %bitcast.place, f32[256,256]{1,0:T(8,128)S(1)} %get-tuple-element.24.power, ...), custom_call_target="tpu_custom_call" | custom-call | flops 8999999488 | bytes 27000000 | tf_op jit(solution)/shard_map/pallas_call | solution.py:271
  51.5 0.0 copy-start
  51.5 1.3 copy-done
  52.8 10.0 %all-to-all-start = ((f32[64,32,256]{2,1,0:T(8,128)}), f32[64,32,256]{2,1,0:T(8,128)S(1)}, u32[]{:S(2)}, u32[]{:S(2)}) async-start(f32[64,32,256]{2,1,0:T(8,128)} %bitcast.7), calls=%async_computation | async-start | bytes 4194304 | tf_op jit(solution)/shard_map/all_to_all | solution.py:335
  62.9 0.1 collective-permute-start.5
  63.0 1.9 %collective-permute-done.5 = f32[2,2,256,128]{3,2,1,0:T(8,128)S(1)} collective-permute-done((f32[2,2,256,128]{3,2,1,0:T(8,128)S(1)}, f32[2,2,256,128]{3,2,1,0:T(8,128)S(1)}, u32[]{:S(2)}, u32[]{:S(2)}) %collective-permute-start.5) | collective-permute-done | bytes 524320 | tf_op jit(solution)/shard_map/ppermute | solution.py:328
  64.8 0.1 add.6.pair
  64.9 3.5 %collective-permute-start.6 = (f32[2,2,256,128]{3,2,1,0:T(8,128)S(1)}, f32[2,2,256,128]{3,2,1,0:T(8,128)S(1)}, u32[]{:S(2)}, u32[]{:S(2)}) collective-permute-start(f32[2,2,256,128]{3,2,1,0:T(8,128)S(1)} %add.6.pair), channel_id=1, source_target_pairs={{0,4},{4,8},{8,12},{12,16},{16,20},{20,24},{24,28},{28,32},{32,36}... | collective-permute-start | bytes 1572872 | tf_op jit(solution)/shard_map/ppermute | solution.py:329
  68.5 28.1 %collective-permute-done.6.got = f32[2,2,256,128]{3,2,1,0:T(8,128)S(1)} collective-permute-done((f32[2,2,256,128]{3,2,1,0:T(8,128)S(1)}, f32[2,2,256,128]{3,2,1,0:T(8,128)S(1)}, u32[]{:S(2)}, u32[]{:S(2)}) %collective-permute-start.6) | collective-permute-done | bytes 524320 | tf_op jit(solution)/shard_map/ppermute | solution.py:329
  96.6 0.8 shard_map.107
  97.3 0.0 all-to-all-done.parts
  97.3 0.1 shard_map.108.share
  97.5 1.0 shard_map.109
  98.5 10.1 %all-to-all-start.1 = ((f32[32,32,256]{2,1,0:T(8,128)}), f32[32,32,256]{2,1,0:T(8,128)S(1)}, u32[]{:S(2)}, u32[]{:S(2)}) async-start(f32[32,32,256]{2,1,0:T(8,128)} %shard_map.109), calls=%async_computation.1 | async-start | bytes 2097152 | tf_op jit(solution)/shard_map/all_to_all | solution.py:338
  108.7 3.2 %collective-permute-start.7 = (f32[2,2,256,128]{3,2,1,0:T(8,128)S(1)}, f32[2,2,256,128]{3,2,1,0:T(8,128)S(1)}, u32[]{:S(2)}, u32[]{:S(2)}) collective-permute-start(f32[2,2,256,128]{3,2,1,0:T(8,128)S(1)} %get-tuple-element.35), channel_id=1, source_target_pairs={{0,2},{1,3},{2,0},{3,1},{4,6},{5,7},{6,4},{7,5},{8,10},{9,11},{10,... | collective-permute-start | bytes 1572872 | tf_op jit(solution)/shard_map/ppermute | solution.py:331
  111.8 22.7 %collective-permute-done.7 = f32[2,2,256,128]{3,2,1,0:T(8,128)S(1)} collective-permute-done((f32[2,2,256,128]{3,2,1,0:T(8,128)S(1)}, f32[2,2,256,128]{3,2,1,0:T(8,128)S(1)}, u32[]{:S(2)}, u32[]{:S(2)}) %collective-permute-start.7) | collective-permute-done | bytes 524320 | tf_op jit(solution)/shard_map/ppermute | solution.py:331
  134.6 0.1 add.7
  134.6 0.8 slice_bitcast_fusion
  135.4 0.0 all-to-all-done.1
  135.4 1.0 copy.13
Async XLA Ops:
  0.6 13.1 %collective-permute-start = (s32[2,2]{1,0:T(2,128)}, s32[2,2]{1,0:T(2,128)S(1)}, u32[]{:S(2)}, u32[]{:S(2)}) collective-permute-start(s32[2,2]{1,0:T(2,128)} %offsets.7), channel_id=1, source_target_pairs={{0,4},{4,8},{8,12},{12,16},{16,20},{20,24},{24,28},{28,32},{32,36}... | collective-permute-start | bytes 56 | tf_op jit(solution)/shard_map/ppermute | solution.py:294
  4.2 27.3 %collective-permute-start.3 = (f32[2,2,256,256]{3,2,1,0:T(8,128)}, f32[2,2,256,256]{3,2,1,0:T(8,128)}, u32[]{:S(2)}, u32[]{:S(2)}) collective-permute-start(f32[2,2,256,256]{3,2,1,0:T(8,128)} %probe.1), channel_id=1, source_target_pairs={{0,18},{1,19},{2,16},{3,17},{4,22},{5,23},{6,20},{7,21},{8,26},{9,... | collective-permute-start | bytes 3145736 | tf_op jit(solution)/shard_map/ppermute | solution.py:293
  8.3 1.2 copy-start.1
  9.6 1.2 copy-start.2
  10.8 0.7 copy-start.3
  11.5 1.2 copy-start.5
  13.7 17.8 %copy-start.4 = (s32[2,2]{1,0:T(2,128)S(1)}, s32[2,2]{1,0:T(2,128)}, u32[]{:S(2)}) copy-start(s32[2,2]{1,0:T(2,128)} %offsets.7) | copy-start | bytes 52
  13.7 17.8 %copy-start.7 = (bf16[6,256,256]{2,1,0:T(8,128)(2,1)S(1)}, bf16[6,256,256]{2,1,0:T(8,128)(2,1)}, u32[]{:S(2)}) copy-start(bf16[6,256,256]{2,1,0:T(8,128)(2,1)} %constant.9.clone.tab_t) | copy-start | bytes 2359300
  13.7 17.8 %copy-start.8 = (bf16[6,256,256]{2,1,0:T(8,128)(2,1)S(1)}, bf16[6,256,256]{2,1,0:T(8,128)(2,1)}, u32[]{:S(2)}) copy-start(bf16[6,256,256]{2,1,0:T(8,128)(2,1)} %constant.8.clone.tab_a) | copy-start | bytes 2359300
  14.3 15.0 %collective-permute-start.1 = (f32[2,2,128,256]{3,2,1,0:T(8,128)S(1)}, f32[2,2,128,256]{3,2,1,0:T(8,128)S(1)}, u32[]{:S(2)}, u32[]{:S(2)}) collective-permute-start(f32[2,2,128,256]{3,2,1,0:T(8,128)S(1)} %shard_map.104), channel_id=1, source_target_pairs={{4,0},{8,4},{12,8},{16,12},{20,16},{24,20},{28,24},{32,28},{36,32}... | collective-permute-start | bytes 1572872 | tf_op jit(solution)/shard_map/ppermute | solution.py:300
  29.3 2.2 %collective-permute-start.2 = (f32[2,2,128,256]{3,2,1,0:T(8,128)S(1)}, f32[2,2,128,256]{3,2,1,0:T(8,128)S(1)}, u32[]{:S(2)}, u32[]{:S(2)}) collective-permute-start(f32[2,2,128,256]{3,2,1,0:T(8,128)S(1)} %collective-permute-done.1.mine), channel_id=1, source_target_pairs={{0,1},{1,0},{2,3},{3,2},{4,5},{5,4},{6,7},{7,6},{8,9},{9,8},{10,11... | collective-permute-start | bytes 1572872 | tf_op jit(solution)/shard_map/ppermute | solution.py:301
  31.5 10.2 %copy-start.6 = (f32[2,256,256]{2,1,0:T(8,128)S(1)}, f32[2,256,256]{2,1,0:T(8,128)}, u32[]{:S(2)}) copy-start(f32[2,256,256]{2,1,0:T(8,128)} %measured.1) | copy-start | bytes 1572868
  39.9 1.8 %collective-permute-start.4 = (f32[256,256]{1,0:T(8,128)S(1)}, f32[256,256]{1,0:T(8,128)S(1)}, u32[]{:S(2)}, u32[]{:S(2)}) collective-permute-start(f32[256,256]{1,0:T(8,128)S(1)} %get-tuple-element.24.power), channel_id=1, source_target_pairs={{0,1},{1,0},{2,3},{3,2},{4,5},{5,4},{6,7},{7,6},{8,9},{9,8},{10,11... | collective-permute-start | bytes 786440 | tf_op jit(solution)/shard_map/ppermute | solution.py:309
  51.5 1.3 copy-start
  52.8 44.5 %all-to-all-start = ((f32[64,32,256]{2,1,0:T(8,128)}), f32[64,32,256]{2,1,0:T(8,128)S(1)}, u32[]{:S(2)}, u32[]{:S(2)}) async-start(f32[64,32,256]{2,1,0:T(8,128)} %bitcast.7), calls=%async_computation | async-start | bytes 4194304 | tf_op jit(solution)/shard_map/all_to_all | solution.py:335
  62.9 2.0 %collective-permute-start.5 = (f32[2,2,256,128]{3,2,1,0:T(8,128)S(1)}, f32[2,2,256,128]{3,2,1,0:T(8,128)S(1)}, u32[]{:S(2)}, u32[]{:S(2)}) collective-permute-start(f32[2,2,256,128]{3,2,1,0:T(8,128)S(1)} %get-tuple-element.33), channel_id=1, source_target_pairs={{0,1},{1,0},{2,3},{3,2},{4,5},{5,4},{6,7},{7,6},{8,9},{9,8},{10,11... | collective-permute-start | bytes 1572872 | tf_op jit(solution)/shard_map/ppermute | solution.py:328
  64.9 31.6 %collective-permute-start.6 = (f32[2,2,256,128]{3,2,1,0:T(8,128)S(1)}, f32[2,2,256,128]{3,2,1,0:T(8,128)S(1)}, u32[]{:S(2)}, u32[]{:S(2)}) collective-permute-start(f32[2,2,256,128]{3,2,1,0:T(8,128)S(1)} %add.6.pair), channel_id=1, source_target_pairs={{0,4},{4,8},{8,12},{12,16},{16,20},{20,24},{24,28},{28,32},{32,36}... | collective-permute-start | bytes 1572872 | tf_op jit(solution)/shard_map/ppermute | solution.py:329
  98.5 36.9 %all-to-all-start.1 = ((f32[32,32,256]{2,1,0:T(8,128)}), f32[32,32,256]{2,1,0:T(8,128)S(1)}, u32[]{:S(2)}, u32[]{:S(2)}) async-start(f32[32,32,256]{2,1,0:T(8,128)} %shard_map.109), calls=%async_computation.1 | async-start | bytes 2097152 | tf_op jit(solution)/shard_map/all_to_all | solution.py:338
  108.7 25.9 %collective-permute-start.7 = (f32[2,2,256,128]{3,2,1,0:T(8,128)S(1)}, f32[2,2,256,128]{3,2,1,0:T(8,128)S(1)}, u32[]{:S(2)}, u32[]{:S(2)}) collective-permute-start(f32[2,2,256,128]{3,2,1,0:T(8,128)S(1)} %get-tuple-element.35), channel_id=1, source_target_pairs={{0,2},{1,3},{2,0},{3,1},{4,6},{5,7},{6,4},{7,5},{8,10},{9,11},{10,... | collective-permute-start | bytes 1572872 | tf_op jit(solution)/shard_map/ppermute | solution.py:331

commit v3 on v2

--- a/solution.py
+++ b/solution.py
@@ -107,11 +107,7 @@
     return lax.broadcasted_iota(jnp.int32, shape, 1) >= offsets[slot, 1]
 
 
-def prepare_kernel(place, offsets, phase, absorb, probe, inside, rolled):
-    on_left = left_of(offsets, place[0] // 2, PLANE)
-    for layer in range(2):
-        for kind, strip in enumerate((phase, absorb)):
-            inside[layer, kind] = jnp.where(on_left, strip[layer, :, :LENGTH], strip[layer, :, LENGTH:])
+def roll_kernel(place, offsets, probe, rolled):
     roll_probes(offsets, place, probe, rolled)
 
 
@@ -123,14 +119,16 @@
             out[layer, kind] = jnp.where(on_left, strip[layer, part, :LENGTH], strip[layer, part, LENGTH:])
 
 
-def slot_transmit(offsets, place, layer, inside, mine, other):
+def slot_transmit(offsets, place, layer, strips, mine, other):
     swap = place[0] % 2 == 1
     in_strip = lax.broadcasted_iota(jnp.int32, PLANE, 0) >= offsets[place[0] // 2, 0]
+    on_left = left_of(offsets, place[0] // 2, PLANE)
     patch = []
     for kind in range(2):
         low = jnp.where(swap, other[layer, kind], mine[layer, kind])
         high = jnp.where(swap, mine[layer, kind], other[layer, kind])
-        patch.append(jnp.where(in_strip, inside[layer, kind], jnp.concatenate([low, high], axis=0)))
+        inside = jnp.where(on_left, strips[kind][layer, :, :LENGTH], strips[kind][layer, :, LENGTH:])
+        patch.append(jnp.where(in_strip, inside, jnp.concatenate([low, high], axis=0)))
     return transmit(*patch)
 
 
@@ -154,11 +152,11 @@
 
 
 def forward_kernel(
-    offsets, place, inside, mine, other, rolled_o, probe_f, tab_a, tab_t,
+    offsets, place, phase, absorb, mine, other, rolled_o, probe_f, tab_a, tab_t,
     rolled_f, wave_o, wave_f, field_o, field_f, trans0, trans1, power,
 ):
-    trans0[0], trans0[1] = slot_transmit(offsets, place, 0, inside, mine, other)
-    trans1[0], trans1[1] = slot_transmit(offsets, place, 1, inside, mine, other)
+    trans0[0], trans0[1] = slot_transmit(offsets, place, 0, (phase, absorb), mine, other)
+    trans1[0], trans1[1] = slot_transmit(offsets, place, 1, (phase, absorb), mine, other)
     roll_probes(offsets, place, probe_f, rolled_f)
     total = None
     for rolled, wave, field in ((rolled_o, wave_o, field_o), (rolled_f, wave_f, field_f)):
@@ -170,7 +168,7 @@
     power[...] = total
 
 
-def adjoint(offsets, place, factor, field, wave, rolled, trans0, trans1, tab_a, tab_t, put):
+def adjoint(offsets, place, factor, field, wave, rolled, trans0, trans1, tab_a, tab_t, grads, which):
     slot = place[0] // 2
     row, column = offsets[slot, 0], offsets[slot, 1]
     back_row, back_column = (LENGTH - row) % LENGTH, (LENGTH - column) % LENGTH
@@ -188,33 +186,27 @@
         -sum(hr * rolled[m, 1] + hi * rolled[m, 0] for m, (hr, hi) in enumerate(back)),
     )
     for m, (hr, hi) in enumerate(back):
-        put(2 * m, roll2(hr * tr - hi * ti, back_row, back_column))
-        put(2 * m + 1, roll2(-(hr * ti + hi * tr), back_row, back_column))
+        for part, value in enumerate((hr * tr - hi * ti, -(hr * ti + hi * tr))):
+            value = roll2(value, back_row, back_column)
+            for i in range(4):
+                grads[4 * (2 * m + part) + i, which] = value[i * CHUNK : (i + 1) * CHUNK]
     return lower, upper
 
 
 def backward_kernel(
     offsets, counts, place, power, near, measured, field_o, field_f, wave_o, wave_f, rolled_o, rolled_f,
-    trans0, trans1, tab_a, tab_t, grads, keep, send, factor, partial, planes, sems,
+    trans0, trans1, tab_a, tab_t, grads, keep, send, factor, partial,
 ):
     slot, swap = place[0] // 2, place[0] % 2 == 1
     valid = (slot < counts[0]).astype(F32)
     target = jnp.where(slot == 1, measured[1], measured[0])
     factor[...] = valid * (1.0 - jnp.sqrt(target + 1.0) / jnp.sqrt(power[...] + near[...] + 1.0))
     rest = (trans0, trans1, tab_a, tab_t)
-    copies = []
-
-    def put(index, value, foreign):
-        planes[foreign, index] = value
-        out = grads.at[jnp.bitwise_xor(slot, foreign), index]
-        copies.append(pltpu.make_async_copy(planes.at[foreign, index], out, sems.at[foreign, index]))
-        copies[-1].start()
-
-    sums = adjoint(offsets, place, factor[...], field_f, wave_f, rolled_f, *rest, functools.partial(put, foreign=1))
+    sums = adjoint(offsets, place, factor[...], field_f, wave_f, rolled_f, *rest, grads, 1)
     for layer in range(2):
         for part in range(2):
             partial[layer, part] = sums[layer][part]
-    sums = adjoint(offsets, place, factor[...], field_o, wave_o, rolled_o, *rest, functools.partial(put, foreign=0))
+    sums = adjoint(offsets, place, factor[...], field_o, wave_o, rolled_o, *rest, grads, 0)
     for layer, trans in enumerate((trans0, trans1)):
         gr, gi = (sums[layer][part] + partial[layer, part] for part in range(2))
         tr, ti = trans[0], trans[1]
@@ -222,36 +214,40 @@
             left, right = grad[:, :HALF], grad[:, HALF:]
             keep[kind, layer] = jnp.where(swap, right, left)
             send[kind, layer] = jnp.where(swap, left, right)
-    for copy in copies:
-        copy.wait()
-
-
-def fold_kernel(offsets, upper_offsets, place, pair, got, mine, send):
+
+
+def fold_kernel(offsets, place, pair, far_pair, own, below):
     core, zhi = place[0] % 2, place[0] // 2
     rows = lax.broadcasted_iota(jnp.int32, (LENGTH, HALF), 0)
     columns = lax.broadcasted_iota(jnp.int32, (LENGTH, HALF), 1) + core * HALF
-    own_rows, upper_rows = rows >= offsets[zhi, 0], rows < upper_offsets[zhi, 0]
-    own_mine = jnp.logical_xor(columns >= offsets[zhi, 1], zhi == 1)
-    upper_mine = jnp.logical_xor(columns >= upper_offsets[zhi, 1], zhi == 1)
+    where = []
+    for slot in (zhi, 1 - zhi):
+        on_mine = jnp.logical_xor(columns >= offsets[slot, 1], zhi == 1)
+        where.append((on_mine, rows >= offsets[slot, 0]))
     for kind in range(2):
         for layer in range(2):
-            own = jnp.where(own_rows, pair[kind, layer], 0.0)
-            upper = jnp.where(upper_rows, got[kind, layer], 0.0)
-            mine[kind, layer] = jnp.where(own_mine, own, 0.0) + jnp.where(upper_mine, upper, 0.0)
-            send[kind, layer] = jnp.where(own_mine, 0.0, own) + jnp.where(upper_mine, 0.0, upper)
-
-
-def sum_kernel(parts, after, out):
+            sums = [0.0, 0.0]
+            for (on_mine, in_strip), source in zip(where, (pair, far_pair)):
+                value = jnp.where(on_mine, source[kind, layer], 0.0)
+                inside = jnp.where(in_strip, value, 0.0)
+                sums = [sums[0] + inside, sums[1] + (value - inside)]
+            own[kind, layer], below[kind, layer] = sums
+
+
+def sum_kernel(parts, after, own, foreign):
     del after
-    total = parts[0]
-    for i in range(1, parts.shape[0]):
-        total += parts[i]
-    out[...] = total
-
-
-def spread_kernel(share, out):
+    for which, out in enumerate((own, foreign)):
+        total = parts[0, which]
+        for i in range(1, parts.shape[0]):
+            total += parts[i, which]
+        out[...] = total
+
+
+def spread_kernel(share, far, after, out):
+    del after
+    total = share[...] + far[...]
     for i in range(out.shape[0]):
-        out[i] = share[...]
+        out[i] = total
 
 
 VMEM = pl.BlockSpec(memory_space=pltpu.VMEM)
@@ -259,11 +255,11 @@
 ANY = pl.BlockSpec(memory_space=pl.ANY)
 HBM = pl.BlockSpec(memory_space=pltpu.HBM)
 PLANE = (LENGTH, LENGTH)
+CHUNKS, CHUNK = 16, 64
 WAVE = (LOCAL_MODES, 2, LENGTH, LENGTH)
 ONE = (1, 2, LENGTH, LENGTH)
 PAIR = (2, LENGTH, LENGTH)
 SHARE = (2, 2, LENGTH, HALF)
-STRIPS = (2, 2, LENGTH, LENGTH)
 HALVES = (2, 2, HALF, LENGTH)
 
 
@@ -287,15 +283,13 @@
     cores = [(i, i ^ 1) for i in range(4)]
     far = [(i, i ^ 2) for i in range(4)]
     flip = [(4 * t + m, 4 * (t ^ 4) + (m ^ 2)) for t in range(TILES) for m in range(4)]
-    holders = [[4 * t + 2 * h + c for h in range(2) for t in range(TILES)] for c in range(2)]
+    planes = [[(x * 2 + z) * 4 + y for x in range(4) for y in range(4)] for z in range(2)]
+    across = [(i, i ^ 4) for i in range(TILES)]
     tab_a, tab_t = (jnp.asarray(t) for t in constant_tables())
 
     foreign = lax.ppermute(probe_modes, ("tile", "mode"), flip)
     upper_offsets = lax.ppermute(offsets, "tile", down)
-    inside, rolled_o = run(
-        prepare_kernel, 1.5, 2, [STRIPS, WAVE], (place, offsets, object_phase, object_absorb, probe_modes)
-    )
-    upper_offsets, inside = lax.optimization_barrier((upper_offsets, inside))
+    (rolled_o,) = run(roll_kernel, 0.05, 2, [WAVE], (place, offsets, probe_modes))
     (pick,) = run(pick_kernel, 0.5, 2, [HALVES], (place, upper_offsets, object_phase, object_absorb))
     mine = lax.ppermute(pick, "tile", up)
     other = lax.ppermute(mine, "mode", cores)
@@ -304,38 +298,33 @@
         8.0,
         2,
         [WAVE] * 5 + [PAIR, PAIR, PLANE],
-        (offsets, place, inside, mine, other, rolled_o, foreign, tab_a, tab_t),
+        (offsets, place, object_phase, object_absorb, mine, other, rolled_o, foreign, tab_a, tab_t),
     )
     near = lax.ppermute(power, "mode", cores)
     grads, keep, send = run(
         backward_kernel,
         9.0,
         3,
-        [(2, 4) + PLANE, SHARE, SHARE],
+        [(CHUNKS, 2, CHUNK, LENGTH), SHARE, SHARE],
         (
             offsets, counts, place, power, near, measured, field_o, field_f, wave_o, wave_f, rolled_o, rolled_f,
             trans0, trans1, tab_a, tab_t,
         ),
-        scratch=[
-            pltpu.VMEM(PLANE, F32),
-            pltpu.VMEM((2, 2) + PLANE, F32),
-            pltpu.VMEM((2, 4) + PLANE, F32),
-            pltpu.SemaphoreType.DMA((2, 4)),
-        ],
-        out_specs=[HBM, VMEM, VMEM],
+        scratch=[pltpu.VMEM(PLANE, F32), pltpu.VMEM((2, 2) + PLANE, F32)],
     )
 
     pair = keep + lax.ppermute(send, "mode", cores)
-    got = lax.ppermute(pair, "tile", down)
-    own, send = run(fold_kernel, 0.05, 3, [SHARE, SHARE], (offsets, upper_offsets, place, pair, got))
-    from_far = lax.ppermute(send, "mode", far)
-    grad_object = own + from_far
-
-    grads = grads.reshape(2 * TILES, -1, LENGTH)
-    parts = lax.all_to_all(grads, ("tile", "mode"), 0, 0, axis_index_groups=holders)
-    (share,) = run(sum_kernel, 0.5, 0, [parts.shape[1:]], (parts, own), [VMEM, ANY])
-    (spread,) = run(spread_kernel, 0.5, 0, [(TILES,) + share.shape], (share,))
-    probe_total = lax.all_to_all(spread, "tile", 0, 0).reshape(WAVE)
+    far_pair = lax.ppermute(pair, "mode", far)
+    own, below = run(fold_kernel, 0.05, 2, [SHARE, SHARE], (offsets, place, pair, far_pair))
+    above = lax.ppermute(below, "tile", down)
+    grad_object = own + above
+
+    parts = lax.all_to_all(grads, "tile", 0, 0, axis_index_groups=planes)
+    share, share_f = run(sum_kernel, 0.5, 0, [(CHUNK, LENGTH)] * 2, (parts, below), [VMEM, ANY])
+    share += lax.ppermute(share_f, ("tile", "mode"), flip)
+    far_share = lax.ppermute(share, "tile", across)
+    (spread,) = run(spread_kernel, 0.5, 0, [(CHUNKS, CHUNK, LENGTH)], (share, far_share, above), [VMEM, VMEM, ANY])
+    probe_total = lax.all_to_all(spread, "tile", 0, 0, axis_index_groups=planes).reshape(WAVE)
     return (grad_object[0], grad_object[1], probe_total)
 
 

time: 137 us -> 124 us (0.905)
  starting transfers between devices: 36.2 us -> 29.4 us
  waiting for transfers between devices: 69.5 us -> 66.4 us
  local copies, waits for them, and re-layouts: 7.5 us -> 5.6 us
    ppermute x2 -> x4, waiting for transfers between devices: 50.8 us -> 20.7 us  [the longest x1 13.9 us: per_device(): far_pair = lax.ppermute(pair, 'mode', far)]
    all_to_all x2, waiting for transfers between devices: 0.01 us -> 25.4 us  [the longest x1 17.1 us: per_device(): lax.all_to_all(spread, 'tile', 0, 0, axis_index_groups=planes).reshape(WAVE)]
    all_to_all x2, starting transfers between devices: 20.2 us -> 11.2 us  [the longest x1 6.73 us: per_device(): parts = lax.all_to_all(grads, 'tile', 0, 0, axis_index_groups=planes)]
    unnamed x19, local copies, waits for them, and re-layouts: 6.67 us -> 4.77 us
    ppermute x2 -> x4, starting transfers between devices: 6.68 us -> 8.54 us  [the longest x1 3.77 us: per_device(): above = lax.ppermute(below, 'tile', down)]
    ppermute x1, waiting for transfers between devices: 2.17 us -> 3.89 us  [per_device(): foreign = lax.ppermute(probe_modes, ('tile', 'mode'), flip)]
  transfers between devices with their start and end apart: 10 -> 12, of which waited for: 6 -> 9; matrix products, arithmetic and copies ran while one was open for 1% -> 1% of each run, Pallas kernels for 2% -> 3%
where the time goes in v3:
time: 124 us; the launch traced here: 123 us
  waiting for transfers between devices  66.4 us (54%)
  starting transfers between devices  29.4 us (24%)
  Pallas kernels  20.4 us (16%)
  local copies, waits for them, and re-layouts  5.6 us (5%)
  between operations  1.45 us (1%)
    pallas_call x7, Pallas kernels, run(): pl.pallas_call(kernel, out_shape=[jax.ShapeDtypeStruct(o, F32) for o in o...  20.4 us
    all_to_all x1, waiting for transfers between devices, per_device(): lax.all_to_all(spread, 'tile', 0, 0, axis_index_groups=planes).reshape(WAVE)  17.1 us
    ppermute x1, waiting for transfers between devices, per_device(): far_pair = lax.ppermute(pair, 'mode', far)  13.9 us
    ppermute x1, waiting for transfers between devices, per_device(): mine = lax.ppermute(pick, 'tile', up)  13.7 us
    all_to_all x1, waiting for transfers between devices, per_device(): parts = lax.all_to_all(grads, 'tile', 0, 0, axis_index_groups=planes)  8.32 us
    all_to_all x1, starting transfers between devices, per_device(): parts = lax.all_to_all(grads, 'tile', 0, 0, axis_index_groups=planes)  6.73 us
    unnamed x19, local copies, waits for them, and re-layouts  4.77 us
    all_to_all x1, starting transfers between devices, per_device(): lax.all_to_all(spread, 'tile', 0, 0, axis_index_groups=planes).reshape(WAVE)  4.5 us
  transfers between devices with their start and end apart: 12, of which 9 were waited for; matrix products, arithmetic and copies ran while one was open for 1% of the time, Pallas kernels for 3%

profile of v3, /device:TPU:0, one launch (start us, length us, event | category | flops | bytes accessed | tf_op | source)
XLA Modules:
  0.0 123.4 jit_solution(257405148435701363)
XLA Ops:
  0.6 0.0 copy-start.1
  0.6 3.7 %collective-permute-start = (s32[2,2]{1,0:T(2,128)}, s32[2,2]{1,0:T(2,128)S(1)}, u32[]{:S(2)}, u32[]{:S(2)}) collective-permute-start(s32[2,2]{1,0:T(2,128)} %offsets.7), channel_id=1, source_target_pairs={{0,4},{4,8},{8,12},{12,16},{16,20},{20,24},{24,28},{28,32},{32,36}... | collective-permute-start | bytes 56 | tf_op jit(solution)/shard_map/ppermute | solution.py:291
  4.3 4.1 %collective-permute-start.3 = (f32[2,2,256,256]{3,2,1,0:T(8,128)}, f32[2,2,256,256]{3,2,1,0:T(8,128)S(1)}, u32[]{:S(2)}, u32[]{:S(2)}) collective-permute-start(f32[2,2,256,256]{3,2,1,0:T(8,128)} %probe.1), channel_id=1, source_target_pairs={{0,18},{1,19},{2,16},{3,17},{4,22},{5,23},{6,20},{7,21},{8,26},{9,... | collective-permute-start | bytes 3145736 | tf_op jit(solution)/shard_map/ppermute | solution.py:290
  8.5 0.0 collective-permute-done.upper_offsets
  8.5 0.0 copy-start.2
  8.5 1.2 copy-done.2
  9.7 0.0 copy-start.3
  9.7 1.2 copy-done.3
  10.9 0.0 copy-start.5
  10.9 0.0 copy-start.4
  10.9 0.0 copy-start.7
  10.9 0.0 copy-start.8
  10.9 0.6 shard_map.103
  11.5 1.4 %collective-permute-start.1 = (f32[2,2,128,256]{3,2,1,0:T(8,128)S(1)}, f32[2,2,128,256]{3,2,1,0:T(8,128)S(1)}, u32[]{:S(2)}, u32[]{:S(2)}) collective-permute-start(f32[2,2,128,256]{3,2,1,0:T(8,128)S(1)} %shard_map.103), channel_id=1, source_target_pairs={{4,0},{8,4},{12,8},{16,12},{20,16},{24,20},{28,24},{32,28},{36,32}... | collective-permute-start | bytes 1572872 | tf_op jit(solution)/shard_map/ppermute | solution.py:294
  13.0 13.7 %collective-permute-done.1.mine = f32[2,2,128,256]{3,2,1,0:T(8,128)S(1)} collective-permute-done((f32[2,2,128,256]{3,2,1,0:T(8,128)S(1)}, f32[2,2,128,256]{3,2,1,0:T(8,128)S(1)}, u32[]{:S(2)}, u32[]{:S(2)}) %collective-permute-start.1) | collective-permute-done | bytes 524320 | tf_op jit(solution)/shard_map/ppermute | solution.py:294
  26.7 0.0 collective-permute-start.2
  26.7 0.0 copy-done.1
  26.7 0.0 copy-done.5
  26.7 1.0 shard_map.104.rolled_o
  27.7 0.0 copy-start.6
  27.7 3.9 %collective-permute-done.3.probe_f = f32[2,2,256,256]{3,2,1,0:T(8,128)S(1)} collective-permute-done((f32[2,2,256,256]{3,2,1,0:T(8,128)}, f32[2,2,256,256]{3,2,1,0:T(8,128)S(1)}, u32[]{:S(2)}, u32[]{:S(2)}) %collective-permute-start.3) | collective-permute-done | bytes 1048608 | tf_op jit(solution)/shard_map/ppermute | solution.py:290
  31.6 0.0 collective-permute-done.2.other
  31.6 0.0 copy-done.4
  31.6 0.0 copy-done.7
  31.6 0.0 copy-done.8
  31.6 7.6 %shard_map.105 = (f32[2,2,256,256]{3,2,1,0:T(8,128)S(1)}, f32[2,2,256,256]{3,2,1,0:T(8,128)S(1)}, f32[2,2,256,256]{3,2,1,0:T(8,128)S(1)}, f32[2,2,256,256]{3,2,1...) custom-call(s32[2,2]{1,0:T(2,128)S(1)} %copy-done.5, ...), custom_call_target="tpu_custom_call" | custom-call | flops 8000000000 | bytes 24000000 | tf_op jit(solution)/shard_map/pallas_call | solution.py:267
  39.2 0.3 collective-permute-start.4
  40.1 0.9 collective-permute-done.4.near
  41.0 0.0 copy-done.6
  41.0 8.5 %shard_map.106 = (f32[16,2,64,256]{3,2,1,0:T(8,128)S(1)}, f32[2,2,256,128]{3,2,1,0:T(8,128)S(1)}, f32[2,2,256,128]{3,2,1,0:T(8,128)S(1)}) custom-call(s32[2,2]{1,0:T(2,128)S(1)} %copy-done.5, s32[1]{0:T(128)S(6)} %copy.12.counts, s32[1]{0:T(128)} %bitcast.place, f32[256,256]{1,0:T(8,128)S(1)} %get-tuple-element.18.power, ...), custom_call_target="tpu_custom_call" | custom-call | flops 8999999488 | bytes 27000000 | tf_op jit(solution)/shard_map/pallas_call | solution.py:267
  49.5 0.0 copy-start
  49.5 1.3 %copy-done = f32[16,2,64,256]{3,2,1,0:T(8,128)} copy-done((f32[16,2,64,256]{3,2,1,0:T(8,128)}, f32[16,2,64,256]{3,2,1,0:T(8,128)S(1)}, u32[]{:S(2)}) %copy-start) | copy-done | bytes 2097176
  50.9 6.7 %all-to-all-start = ((f32[16,2,64,256]{3,2,1,0:T(8,128)}), f32[16,2,64,256]{3,2,1,0:T(8,128)S(1)}, u32[]{:S(2)}, u32[]{:S(2)}) async-start(f32[16,2,64,256]{3,2,1,0:T(8,128)} %copy-done), calls=%async_computation | async-start | bytes 4194304 | tf_op jit(solution)/shard_map/all_to_all | solution.py:322
  57.6 0.1 collective-permute-start.5
  57.7 1.9 %collective-permute-done.5 = f32[2,2,256,128]{3,2,1,0:T(8,128)S(1)} collective-permute-done((f32[2,2,256,128]{3,2,1,0:T(8,128)S(1)}, f32[2,2,256,128]{3,2,1,0:T(8,128)S(1)}, u32[]{:S(2)}, u32[]{:S(2)}) %collective-permute-start.5) | collective-permute-done | bytes 524320 | tf_op jit(solution)/shard_map/ppermute | solution.py:316
  59.6 0.1 add.9.pair
  59.7 1.7 %collective-permute-start.6 = (f32[2,2,256,128]{3,2,1,0:T(8,128)S(1)}, f32[2,2,256,128]{3,2,1,0:T(8,128)S(1)}, u32[]{:S(2)}, u32[]{:S(2)}) collective-permute-start(f32[2,2,256,128]{3,2,1,0:T(8,128)S(1)} %add.9.pair), channel_id=1, source_target_pairs={{0,2},{1,3},{2,0},{3,1},{4,6},{5,7},{6,4},{7,5},{8,10},{9,11},{10,... | collective-permute-start | bytes 1572872 | tf_op jit(solution)/shard_map/ppermute | solution.py:317
  61.3 13.9 %collective-permute-done.6.far_pair = f32[2,2,256,128]{3,2,1,0:T(8,128)S(1)} collective-permute-done((f32[2,2,256,128]{3,2,1,0:T(8,128)S(1)}, f32[2,2,256,128]{3,2,1,0:T(8,128)S(1)}, u32[]{:S(2)}, u32[]{:S(2)}) %collective-permute-start.6) | collective-permute-done | bytes 524320 | tf_op jit(solution)/shard_map/ppermute | solution.py:317
  75.2 1.5 %shard_map.107 = (f32[2,2,256,128]{3,2,1,0:T(8,128)S(1)}, f32[2,2,256,128]{3,2,1,0:T(8,128)}) custom-call(s32[2,2]{1,0:T(2,128)S(1)} %copy-done.5, s32[1]{0:T(128)} %bitcast.place, f32[2,2,256,128]{3,2,1,0:T(8,128)S(1)} %add.9.pair, f32[2,2,256,128]{3,2,1,0:T(8,128)S(1)} %collective-permute-done.6.far_pair), custom_call_target="tpu_custom_call" | custom-call | flops 50000000 | bytes 150000 | tf_op jit(solution)/shard_map/pallas_call | solution.py:267
  76.8 3.8 %collective-permute-start.7 = (f32[2,2,256,128]{3,2,1,0:T(8,128)}, f32[2,2,256,128]{3,2,1,0:T(8,128)S(1)}, u32[]{:S(2)}, u32[]{:S(2)}) collective-permute-start(f32[2,2,256,128]{3,2,1,0:T(8,128)} %get-tuple-element.29.after), channel_id=1, source_target_pairs={{0,4},{4,8},{8,12},{12,16},{16,20},{20,24},{24,28},{28,32},{32,36}... | collective-permute-start | bytes 1572872 | tf_op jit(solution)/shard_map/ppermute | solution.py:319
  80.5 8.3 %all-to-all-done.parts = f32[16,2,64,256]{3,2,1,0:T(8,128)S(1)} async-done(((f32[16,2,64,256]{3,2,1,0:T(8,128)}), f32[16,2,64,256]{3,2,1,0:T(8,128)S(1)}, u32[]{:S(2)}, u32[]{:S(2)}) %all-to-all-start) | async-done | bytes 2097184 | tf_op jit(solution)/shard_map/all_to_all | solution.py:322
  88.8 0.1 shard_map.108
  89.0 3.0 %collective-permute-start.8 = (f32[64,256]{1,0:T(8,128)S(1)}, f32[64,256]{1,0:T(8,128)S(1)}, u32[]{:S(2)}, u32[]{:S(2)}) collective-permute-start(f32[64,256]{1,0:T(8,128)S(1)} %get-tuple-element.32), channel_id=1, source_target_pairs={{0,18},{1,19},{2,16},{3,17},{4,22},{5,23},{6,20},{7,21},{8,26},{9,... | collective-permute-start | bytes 196616 | tf_op jit(solution)/shard_map/ppermute | solution.py:324
  92.0 2.5 %collective-permute-done.8 = f32[64,256]{1,0:T(8,128)S(1)} collective-permute-done((f32[64,256]{1,0:T(8,128)S(1)}, f32[64,256]{1,0:T(8,128)S(1)}, u32[]{:S(2)}, u32[]{:S(2)}) %collective-permute-start.8) | collective-permute-done | bytes 65568 | tf_op jit(solution)/shard_map/ppermute | solution.py:324
  94.5 0.1 collective-permute-start.9
  94.6 0.0 collective-permute-done.7.after
  94.6 4.2 %collective-permute-done.9.far = f32[64,256]{1,0:T(8,128)S(1)} collective-permute-done((f32[64,256]{1,0:T(8,128)S(1)}, f32[64,256]{1,0:T(8,128)S(1)}, u32[]{:S(2)}, u32[]{:S(2)}) %collective-permute-start.9) | collective-permute-done | bytes 65568 | tf_op jit(solution)/shard_map/ppermute | solution.py:325
  98.9 1.1 shard_map.109
  99.9 4.5 %all-to-all-start.1 = ((f32[16,64,256]{2,1,0:T(8,128)}), f32[16,64,256]{2,1,0:T(8,128)S(1)}, u32[]{:S(2)}, u32[]{:S(2)}) async-start(f32[16,64,256]{2,1,0:T(8,128)} %shard_map.109), calls=%async_computation.1 | async-start | bytes 2097152 | tf_op jit(solution)/shard_map/all_to_all | solution.py:327
  104.5 0.1 add.10
  104.5 0.8 slice_bitcast_fusion
  105.3 17.1 %all-to-all-done.1 = f32[16,64,256]{2,1,0:T(8,128)S(1)} async-done(((f32[16,64,256]{2,1,0:T(8,128)}), f32[16,64,256]{2,1,0:T(8,128)S(1)}, u32[]{:S(2)}, u32[]{:S(2)}) %all-to-all-start.1) | async-done | bytes 1048608 | tf_op jit(solution)/shard_map/all_to_all | solution.py:327
  122.4 1.0 copy.13
  (1 shorter events, 0.0 us)
Async XLA Ops:
  0.6 26.1 %copy-start.1 = (f32[2,2,256,256]{3,2,1,0:T(8,128)S(1)}, f32[2,2,256,256]{3,2,1,0:T(8,128)}, u32[]{:S(2)}) copy-start(f32[2,2,256,256]{3,2,1,0:T(8,128)} %probe.1) | copy-start | bytes 3145732
  0.6 7.8 %collective-permute-start = (s32[2,2]{1,0:T(2,128)}, s32[2,2]{1,0:T(2,128)S(1)}, u32[]{:S(2)}, u32[]{:S(2)}) collective-permute-start(s32[2,2]{1,0:T(2,128)} %offsets.7), channel_id=1, source_target_pairs={{0,4},{4,8},{8,12},{12,16},{16,20},{20,24},{24,28},{28,32},{32,36}... | collective-permute-start | bytes 56 | tf_op jit(solution)/shard_map/ppermute | solution.py:291
  4.3 27.2 %collective-permute-start.3 = (f32[2,2,256,256]{3,2,1,0:T(8,128)}, f32[2,2,256,256]{3,2,1,0:T(8,128)S(1)}, u32[]{:S(2)}, u32[]{:S(2)}) collective-permute-start(f32[2,2,256,256]{3,2,1,0:T(8,128)} %probe.1), channel_id=1, source_target_pairs={{0,18},{1,19},{2,16},{3,17},{4,22},{5,23},{6,20},{7,21},{8,26},{9,... | collective-permute-start | bytes 3145736 | tf_op jit(solution)/shard_map/ppermute | solution.py:290
  8.5 1.2 copy-start.2
  9.7 1.2 copy-start.3
  10.9 15.8 %copy-start.5 = (s32[2,2]{1,0:T(2,128)S(1)}, s32[2,2]{1,0:T(2,128)}, u32[]{:S(2)}) copy-start(s32[2,2]{1,0:T(2,128)} %offsets.7) | copy-start | bytes 52
  10.9 20.6 %copy-start.4 = (f32[2,256,512]{2,1,0:T(8,128)S(1)}, f32[2,256,512]{2,1,0:T(8,128)}, u32[]{:S(2)}) copy-start(f32[2,256,512]{2,1,0:T(8,128)} %absorb.3) | copy-start | bytes 3145732
  10.9 20.6 %copy-start.7 = (bf16[6,256,256]{2,1,0:T(8,128)(2,1)S(1)}, bf16[6,256,256]{2,1,0:T(8,128)(2,1)}, u32[]{:S(2)}) copy-start(bf16[6,256,256]{2,1,0:T(8,128)(2,1)} %constant.9.clone.tab_t) | copy-start | bytes 2359300
  10.9 20.6 %copy-start.8 = (bf16[6,256,256]{2,1,0:T(8,128)(2,1)S(1)}, bf16[6,256,256]{2,1,0:T(8,128)(2,1)}, u32[]{:S(2)}) copy-start(bf16[6,256,256]{2,1,0:T(8,128)(2,1)} %constant.8.clone.tab_a) | copy-start | bytes 2359300
  11.5 15.1 %collective-permute-start.1 = (f32[2,2,128,256]{3,2,1,0:T(8,128)S(1)}, f32[2,2,128,256]{3,2,1,0:T(8,128)S(1)}, u32[]{:S(2)}, u32[]{:S(2)}) collective-permute-start(f32[2,2,128,256]{3,2,1,0:T(8,128)S(1)} %shard_map.103), channel_id=1, source_target_pairs={{4,0},{8,4},{12,8},{16,12},{20,16},{24,20},{28,24},{32,28},{36,32}... | collective-permute-start | bytes 1572872 | tf_op jit(solution)/shard_map/ppermute | solution.py:294
  26.7 4.9 %collective-permute-start.2 = (f32[2,2,128,256]{3,2,1,0:T(8,128)S(1)}, f32[2,2,128,256]{3,2,1,0:T(8,128)S(1)}, u32[]{:S(2)}, u32[]{:S(2)}) collective-permute-start(f32[2,2,128,256]{3,2,1,0:T(8,128)S(1)} %collective-permute-done.1.mine), channel_id=1, source_target_pairs={{0,1},{1,0},{2,3},{3,2},{4,5},{5,4},{6,7},{7,6},{8,9},{9,8},{10,11... | collective-permute-start | bytes 1572872 | tf_op jit(solution)/shard_map/ppermute | solution.py:295
  27.7 13.4 %copy-start.6 = (f32[2,256,256]{2,1,0:T(8,128)S(1)}, f32[2,256,256]{2,1,0:T(8,128)}, u32[]{:S(2)}) copy-start(f32[2,256,256]{2,1,0:T(8,128)} %measured.1) | copy-start | bytes 1572868
  39.2 1.8 %collective-permute-start.4 = (f32[256,256]{1,0:T(8,128)S(1)}, f32[256,256]{1,0:T(8,128)S(1)}, u32[]{:S(2)}, u32[]{:S(2)}) collective-permute-start(f32[256,256]{1,0:T(8,128)S(1)} %get-tuple-element.18.power), channel_id=1, source_target_pairs={{0,1},{1,0},{2,3},{3,2},{4,5},{5,4},{6,7},{7,6},{8,9},{9,8},{10,11... | collective-permute-start | bytes 786440 | tf_op jit(solution)/shard_map/ppermute | solution.py:303
  49.5 1.3 %copy-start = (f32[16,2,64,256]{3,2,1,0:T(8,128)}, f32[16,2,64,256]{3,2,1,0:T(8,128)S(1)}, u32[]{:S(2)}) copy-start(f32[16,2,64,256]{3,2,1,0:T(8,128)S(1)} %get-tuple-element.30) | copy-start | bytes 6291460
  50.9 38.0 %all-to-all-start = ((f32[16,2,64,256]{3,2,1,0:T(8,128)}), f32[16,2,64,256]{3,2,1,0:T(8,128)S(1)}, u32[]{:S(2)}, u32[]{:S(2)}) async-start(f32[16,2,64,256]{3,2,1,0:T(8,128)} %copy-done), calls=%async_computation | async-start | bytes 4194304 | tf_op jit(solution)/shard_map/all_to_all | solution.py:322
  57.6 2.0 %collective-permute-start.5 = (f32[2,2,256,128]{3,2,1,0:T(8,128)S(1)}, f32[2,2,256,128]{3,2,1,0:T(8,128)S(1)}, u32[]{:S(2)}, u32[]{:S(2)}) collective-permute-start(f32[2,2,256,128]{3,2,1,0:T(8,128)S(1)} %get-tuple-element.27), channel_id=1, source_target_pairs={{0,1},{1,0},{2,3},{3,2},{4,5},{5,4},{6,7},{7,6},{8,9},{9,8},{10,11... | collective-permute-start | bytes 1572872 | tf_op jit(solution)/shard_map/ppermute | solution.py:316
  59.7 15.5 %collective-permute-start.6 = (f32[2,2,256,128]{3,2,1,0:T(8,128)S(1)}, f32[2,2,256,128]{3,2,1,0:T(8,128)S(1)}, u32[]{:S(2)}, u32[]{:S(2)}) collective-permute-start(f32[2,2,256,128]{3,2,1,0:T(8,128)S(1)} %add.9.pair), channel_id=1, source_target_pairs={{0,2},{1,3},{2,0},{3,1},{4,6},{5,7},{6,4},{7,5},{8,10},{9,11},{10,... | collective-permute-start | bytes 1572872 | tf_op jit(solution)/shard_map/ppermute | solution.py:317
  76.8 17.9 %collective-permute-start.7 = (f32[2,2,256,128]{3,2,1,0:T(8,128)}, f32[2,2,256,128]{3,2,1,0:T(8,128)S(1)}, u32[]{:S(2)}, u32[]{:S(2)}) collective-permute-start(f32[2,2,256,128]{3,2,1,0:T(8,128)} %get-tuple-element.29.after), channel_id=1, source_target_pairs={{0,4},{4,8},{8,12},{12,16},{16,20},{20,24},{24,28},{28,32},{32,36}... | collective-permute-start | bytes 1572872 | tf_op jit(solution)/shard_map/ppermute | solution.py:319
  89.0 5.6 %collective-permute-start.8 = (f32[64,256]{1,0:T(8,128)S(1)}, f32[64,256]{1,0:T(8,128)S(1)}, u32[]{:S(2)}, u32[]{:S(2)}) collective-permute-start(f32[64,256]{1,0:T(8,128)S(1)} %get-tuple-element.32), channel_id=1, source_target_pairs={{0,18},{1,19},{2,16},{3,17},{4,22},{5,23},{6,20},{7,21},{8,26},{9,... | collective-permute-start | bytes 196616 | tf_op jit(solution)/shard_map/ppermute | solution.py:324
  94.5 4.3 %collective-permute-start.9 = (f32[64,256]{1,0:T(8,128)S(1)}, f32[64,256]{1,0:T(8,128)S(1)}, u32[]{:S(2)}, u32[]{:S(2)}) collective-permute-start(f32[64,256]{1,0:T(8,128)S(1)} %add.11.share), channel_id=1, source_target_pairs={{0,16},{4,20},{8,24},{12,28},{16,0},{20,4},{24,8},{28,12},{32,48},... | collective-permute-start | bytes 196616 | tf_op jit(solution)/shard_map/ppermute | solution.py:325
  99.9 22.5 %all-to-all-start.1 = ((f32[16,64,256]{2,1,0:T(8,128)}), f32[16,64,256]{2,1,0:T(8,128)S(1)}, u32[]{:S(2)}, u32[]{:S(2)}) async-start(f32[16,64,256]{2,1,0:T(8,128)} %shard_map.109), calls=%async_computation.1 | async-start | bytes 2097152 | tf_op jit(solution)/shard_map/all_to_all | solution.py:327

commit v4 on v3

--- a/solution.py
+++ b/solution.py
@@ -216,26 +216,22 @@
             send[kind, layer] = jnp.where(swap, left, right)
 
 
-def fold_kernel(offsets, place, pair, far_pair, own, below):
+def fold_kernel(offsets, upper_offsets, place, pair, got, mine, send):
     core, zhi = place[0] % 2, place[0] // 2
     rows = lax.broadcasted_iota(jnp.int32, (LENGTH, HALF), 0)
     columns = lax.broadcasted_iota(jnp.int32, (LENGTH, HALF), 1) + core * HALF
-    where = []
-    for slot in (zhi, 1 - zhi):
-        on_mine = jnp.logical_xor(columns >= offsets[slot, 1], zhi == 1)
-        where.append((on_mine, rows >= offsets[slot, 0]))
+    own_rows, upper_rows = rows >= offsets[zhi, 0], rows < upper_offsets[zhi, 0]
+    own_mine = jnp.logical_xor(columns >= offsets[zhi, 1], zhi == 1)
+    upper_mine = jnp.logical_xor(columns >= upper_offsets[zhi, 1], zhi == 1)
     for kind in range(2):
         for layer in range(2):
-            sums = [0.0, 0.0]
-            for (on_mine, in_strip), source in zip(where, (pair, far_pair)):
-                value = jnp.where(on_mine, source[kind, layer], 0.0)
-                inside = jnp.where(in_strip, value, 0.0)
-                sums = [sums[0] + inside, sums[1] + (value - inside)]
-            own[kind, layer], below[kind, layer] = sums
-
-
-def sum_kernel(parts, after, own, foreign):
-    del after
+            own = jnp.where(own_rows, pair[kind, layer], 0.0)
+            upper = jnp.where(upper_rows, got[kind, layer], 0.0)
+            mine[kind, layer] = jnp.where(own_mine, own, 0.0) + jnp.where(upper_mine, upper, 0.0)
+            send[kind, layer] = jnp.where(own_mine, 0.0, own) + jnp.where(upper_mine, 0.0, upper)
+
+
+def sum_kernel(parts, own, foreign):
     for which, out in enumerate((own, foreign)):
         total = parts[0, which]
         for i in range(1, parts.shape[0]):
@@ -243,8 +239,7 @@
         out[...] = total
 
 
-def spread_kernel(share, far, after, out):
-    del after
+def spread_kernel(share, far, out):
     total = share[...] + far[...]
     for i in range(out.shape[0]):
         out[i] = total
@@ -314,16 +309,16 @@
     )
 
     pair = keep + lax.ppermute(send, "mode", cores)
-    far_pair = lax.ppermute(pair, "mode", far)
-    own, below = run(fold_kernel, 0.05, 2, [SHARE, SHARE], (offsets, place, pair, far_pair))
-    above = lax.ppermute(below, "tile", down)
-    grad_object = own + above
+    got = lax.ppermute(pair, "tile", down)
+    own, send = run(fold_kernel, 0.05, 3, [SHARE, SHARE], (offsets, upper_offsets, place, pair, got))
+    from_far = lax.ppermute(send, "mode", far)
+    grad_object = own + from_far
 
     parts = lax.all_to_all(grads, "tile", 0, 0, axis_index_groups=planes)
-    share, share_f = run(sum_kernel, 0.5, 0, [(CHUNK, LENGTH)] * 2, (parts, below), [VMEM, ANY])
+    share, share_f = run(sum_kernel, 0.5, 0, [(CHUNK, LENGTH)] * 2, (parts,))
     share += lax.ppermute(share_f, ("tile", "mode"), flip)
     far_share = lax.ppermute(share, "tile", across)
-    (spread,) = run(spread_kernel, 0.5, 0, [(CHUNKS, CHUNK, LENGTH)], (share, far_share, above), [VMEM, VMEM, ANY])
+    (spread,) = run(spread_kernel, 0.5, 0, [(CHUNKS, CHUNK, LENGTH)], (share, far_share))
     probe_total = lax.all_to_all(spread, "tile", 0, 0, axis_index_groups=planes).reshape(WAVE)
     return (grad_object[0], grad_object[1], probe_total)
 

time: 124 us -> 122 us (0.984)
  waiting for transfers between devices: 66.4 us -> 64.4 us
    all_to_all x1, waiting for transfers between devices: 17.1 us -> 0.01 us  [per_device(): lax.all_to_all(spread, 'tile', 0, 0, axis_index_groups=planes).reshape(WAVE)]
    all_to_all x1, waiting for transfers between devices: 8.32 us -> 25.4 us  [per_device(): parts = lax.all_to_all(grads, 'tile', 0, 0, axis_index_groups=planes)]
    ppermute x2, waiting for transfers between devices: 13.9 us -> 11.8 us  [the longest x1 11.8 us: per_device(): from_far = lax.ppermute(send, 'mode', far)]
    ppermute x2, starting transfers between devices: 5.43 us -> 6.83 us  [the longest x1 3.78 us: per_device(): got = lax.ppermute(pair, 'tile', down)]
  transfers between devices with their start and end apart: 12 -> 12, of which waited for: 9 -> 8; matrix products, arithmetic and copies ran while one was open for 1% -> 1% of each run, Pallas kernels for 3% -> 3%
where the time goes in v4:
time: 122 us
  waiting for transfers between devices  64.4 us (53%)
  starting transfers between devices  29.9 us (25%)
  Pallas kernels  20 us (16%)
  local copies, waits for them, and re-layouts  5.59 us (5%)
  between operations  1.45 us (1%)
    all_to_all x1, waiting for transfers between devices, per_device(): parts = lax.all_to_all(grads, 'tile', 0, 0, axis_index_groups=planes)  25.4 us
    pallas_call x7, Pallas kernels, run(): pl.pallas_call(kernel, out_shape=[jax.ShapeDtypeStruct(o, F32) for o in o...  20 us
    ppermute x1, waiting for transfers between devices, per_device(): mine = lax.ppermute(pick, 'tile', up)  13.7 us
    ppermute x1, waiting for transfers between devices, per_device(): from_far = lax.ppermute(send, 'mode', far)  11.8 us
    all_to_all x1, starting transfers between devices, per_device(): parts = lax.all_to_all(grads, 'tile', 0, 0, axis_index_groups=planes)  6.74 us
    unnamed x19, local copies, waits for them, and re-layouts  4.77 us
    ppermute x1, waiting for transfers between devices, per_device(): far_share = lax.ppermute(share, 'tile', across)  4.25 us
    ppermute x1, starting transfers between devices, per_device(): foreign = lax.ppermute(probe_modes, ('tile', 'mode'), flip)  4.12 us
  transfers between devices with their start and end apart: 12, of which 8 were waited for; matrix products, arithmetic and copies ran while one was open for 1% of the time, Pallas kernels for 3%

profile of v4, /device:TPU:0, one launch (start us, length us, event | category | flops | bytes accessed | tf_op | source)
XLA Modules:
  0.0 121.5 jit_solution(18119131467410108226)
XLA Ops:
  0.6 0.0 copy-start.1
  0.6 3.7 %collective-permute-start = (s32[2,2]{1,0:T(2,128)}, s32[2,2]{1,0:T(2,128)S(1)}, u32[]{:S(2)}, u32[]{:S(2)}) collective-permute-start(s32[2,2]{1,0:T(2,128)} %offsets.7), channel_id=1, source_target_pairs={{0,4},{4,8},{8,12},{12,16},{16,20},{20,24},{24,28},{28,32},{32,36}... | collective-permute-start | bytes 56 | tf_op jit(solution)/shard_map/ppermute | solution.py:286
  4.3 4.1 %collective-permute-start.3 = (f32[2,2,256,256]{3,2,1,0:T(8,128)}, f32[2,2,256,256]{3,2,1,0:T(8,128)S(1)}, u32[]{:S(2)}, u32[]{:S(2)}) collective-permute-start(f32[2,2,256,256]{3,2,1,0:T(8,128)} %probe.1), channel_id=1, source_target_pairs={{0,18},{1,19},{2,16},{3,17},{4,22},{5,23},{6,20},{7,21},{8,26},{9,... | collective-permute-start | bytes 3145736 | tf_op jit(solution)/shard_map/ppermute | solution.py:285
  8.5 0.0 collective-permute-done.upper_offsets
  8.5 0.0 copy-start.2
  8.5 1.2 %copy-done.2 = f32[2,256,512]{2,1,0:T(8,128)S(1)} copy-done((f32[2,256,512]{2,1,0:T(8,128)S(1)}, f32[2,256,512]{2,1,0:T(8,128)}, u32[]{:S(2)}) %copy-start.2) | copy-done | bytes 1048600
  9.7 0.0 copy-start.3
  9.7 1.2 %copy-done.3 = f32[2,256,512]{2,1,0:T(8,128)S(1)} copy-done((f32[2,256,512]{2,1,0:T(8,128)S(1)}, f32[2,256,512]{2,1,0:T(8,128)}, u32[]{:S(2)}) %copy-start.3) | copy-done | bytes 1048600
  10.9 0.0 copy-start.5
  10.9 0.0 copy-start.4
  10.9 0.0 copy-start.7
  10.9 0.0 copy-start.8
  10.9 0.6 shard_map.103
  11.5 1.4 %collective-permute-start.1 = (f32[2,2,128,256]{3,2,1,0:T(8,128)S(1)}, f32[2,2,128,256]{3,2,1,0:T(8,128)S(1)}, u32[]{:S(2)}, u32[]{:S(2)}) collective-permute-start(f32[2,2,128,256]{3,2,1,0:T(8,128)S(1)} %shard_map.103), channel_id=1, source_target_pairs={{4,0},{8,4},{12,8},{16,12},{20,16},{24,20},{28,24},{32,28},{36,32}... | collective-permute-start | bytes 1572872 | tf_op jit(solution)/shard_map/ppermute | solution.py:289
  13.0 13.7 %collective-permute-done.1.mine = f32[2,2,128,256]{3,2,1,0:T(8,128)S(1)} collective-permute-done((f32[2,2,128,256]{3,2,1,0:T(8,128)S(1)}, f32[2,2,128,256]{3,2,1,0:T(8,128)S(1)}, u32[]{:S(2)}, u32[]{:S(2)}) %collective-permute-start.1) | collective-permute-done | bytes 524320 | tf_op jit(solution)/shard_map/ppermute | solution.py:289
  26.7 0.0 collective-permute-start.2
  26.7 0.0 copy-done.1
  26.7 0.0 copy-done.5
  26.7 1.0 shard_map.104.rolled_o
  27.7 0.0 copy-start.6
  27.7 3.9 %collective-permute-done.3.probe_f = f32[2,2,256,256]{3,2,1,0:T(8,128)S(1)} collective-permute-done((f32[2,2,256,256]{3,2,1,0:T(8,128)}, f32[2,2,256,256]{3,2,1,0:T(8,128)S(1)}, u32[]{:S(2)}, u32[]{:S(2)}) %collective-permute-start.3) | collective-permute-done | bytes 1048608 | tf_op jit(solution)/shard_map/ppermute | solution.py:285
  31.6 0.0 collective-permute-done.2.other
  31.6 0.0 copy-done.4
  31.6 0.0 copy-done.7
  31.6 0.0 copy-done.8
  31.6 7.8 %shard_map.105 = (f32[2,2,256,256]{3,2,1,0:T(8,128)S(1)}, f32[2,2,256,256]{3,2,1,0:T(8,128)S(1)}, f32[2,2,256,256]{3,2,1,0:T(8,128)S(1)}, f32[2,2,256,256]{3,2,1...) custom-call(s32[2,2]{1,0:T(2,128)S(1)} %copy-done.5, ...), custom_call_target="tpu_custom_call" | custom-call | flops 8000000000 | bytes 24000000 | tf_op jit(solution)/shard_map/pallas_call | solution.py:262
  39.4 0.3 collective-permute-start.4
  40.3 0.9 collective-permute-done.4.near
  41.2 0.0 copy-done.6
  41.2 8.7 %shard_map.106 = (f32[16,2,64,256]{3,2,1,0:T(8,128)S(1)}, f32[2,2,256,128]{3,2,1,0:T(8,128)S(1)}, f32[2,2,256,128]{3,2,1,0:T(8,128)S(1)}) custom-call(s32[2,2]{1,0:T(2,128)S(1)} %copy-done.5, s32[1]{0:T(128)S(6)} %copy.12.counts, s32[1]{0:T(128)} %bitcast.place, f32[256,256]{1,0:T(8,128)S(1)} %get-tuple-element.18.power, ...), custom_call_target="tpu_custom_call" | custom-call | flops 8999999488 | bytes 27000000 | tf_op jit(solution)/shard_map/pallas_call | solution.py:262
  49.9 0.0 copy-start
  49.9 1.3 %copy-done = f32[16,2,64,256]{3,2,1,0:T(8,128)} copy-done((f32[16,2,64,256]{3,2,1,0:T(8,128)}, f32[16,2,64,256]{3,2,1,0:T(8,128)S(1)}, u32[]{:S(2)}) %copy-start) | copy-done | bytes 2097176
  51.2 6.7 %all-to-all-start = ((f32[16,2,64,256]{3,2,1,0:T(8,128)}), f32[16,2,64,256]{3,2,1,0:T(8,128)S(1)}, u32[]{:S(2)}, u32[]{:S(2)}) async-start(f32[16,2,64,256]{3,2,1,0:T(8,128)} %copy-done), calls=%async_computation | async-start | bytes 4194304 | tf_op jit(solution)/shard_map/all_to_all | solution.py:317
  58.0 0.1 collective-permute-start.5
  58.0 1.9 %collective-permute-done.5 = f32[2,2,256,128]{3,2,1,0:T(8,128)S(1)} collective-permute-done((f32[2,2,256,128]{3,2,1,0:T(8,128)S(1)}, f32[2,2,256,128]{3,2,1,0:T(8,128)S(1)}, u32[]{:S(2)}, u32[]{:S(2)}) %collective-permute-start.5) | collective-permute-done | bytes 524320 | tf_op jit(solution)/shard_map/ppermute | solution.py:311
  59.9 0.1 add.9.pair
  60.0 3.8 %collective-permute-start.6 = (f32[2,2,256,128]{3,2,1,0:T(8,128)S(1)}, f32[2,2,256,128]{3,2,1,0:T(8,128)S(1)}, u32[]{:S(2)}, u32[]{:S(2)}) collective-permute-start(f32[2,2,256,128]{3,2,1,0:T(8,128)S(1)} %add.9.pair), channel_id=1, source_target_pairs={{0,4},{4,8},{8,12},{12,16},{16,20},{20,24},{24,28},{28,32},{32,36}... | collective-permute-start | bytes 1572872 | tf_op jit(solution)/shard_map/ppermute | solution.py:312
  63.8 25.4 %all-to-all-done.parts = f32[16,2,64,256]{3,2,1,0:T(8,128)S(1)} async-done(((f32[16,2,64,256]{3,2,1,0:T(8,128)}), f32[16,2,64,256]{3,2,1,0:T(8,128)S(1)}, u32[]{:S(2)}, u32[]{:S(2)}) %all-to-all-start) | async-done | bytes 2097184 | tf_op jit(solution)/shard_map/all_to_all | solution.py:317
  89.2 0.1 shard_map.108
  89.3 3.0 %collective-permute-start.8 = (f32[64,256]{1,0:T(8,128)S(1)}, f32[64,256]{1,0:T(8,128)S(1)}, u32[]{:S(2)}, u32[]{:S(2)}) collective-permute-start(f32[64,256]{1,0:T(8,128)S(1)} %get-tuple-element.32), channel_id=1, source_target_pairs={{0,18},{1,19},{2,16},{3,17},{4,22},{5,23},{6,20},{7,21},{8,26},{9,... | collective-permute-start | bytes 196616 | tf_op jit(solution)/shard_map/ppermute | solution.py:319
  92.3 2.5 %collective-permute-done.8 = f32[64,256]{1,0:T(8,128)S(1)} collective-permute-done((f32[64,256]{1,0:T(8,128)S(1)}, f32[64,256]{1,0:T(8,128)S(1)}, u32[]{:S(2)}, u32[]{:S(2)}) %collective-permute-start.8) | collective-permute-done | bytes 65568 | tf_op jit(solution)/shard_map/ppermute | solution.py:319
  94.9 0.1 collective-permute-start.9
  95.0 4.3 %collective-permute-done.9.far = f32[64,256]{1,0:T(8,128)S(1)} collective-permute-done((f32[64,256]{1,0:T(8,128)S(1)}, f32[64,256]{1,0:T(8,128)S(1)}, u32[]{:S(2)}, u32[]{:S(2)}) %collective-permute-start.9) | collective-permute-done | bytes 65568 | tf_op jit(solution)/shard_map/ppermute | solution.py:320
  99.2 1.1 shard_map.109
  100.3 3.7 %all-to-all-start.1 = ((f32[16,64,256]{2,1,0:T(8,128)}), f32[16,64,256]{2,1,0:T(8,128)S(1)}, u32[]{:S(2)}, u32[]{:S(2)}) async-start(f32[16,64,256]{2,1,0:T(8,128)} %shard_map.109), calls=%async_computation.1 | async-start | bytes 2097152 | tf_op jit(solution)/shard_map/all_to_all | solution.py:322
  104.0 0.0 collective-permute-done.6.got
  104.0 0.8 shard_map.107
  104.8 3.1 %collective-permute-start.7 = (f32[2,2,256,128]{3,2,1,0:T(8,128)S(1)}, f32[2,2,256,128]{3,2,1,0:T(8,128)S(1)}, u32[]{:S(2)}, u32[]{:S(2)}) collective-permute-start(f32[2,2,256,128]{3,2,1,0:T(8,128)S(1)} %get-tuple-element.29), channel_id=1, source_target_pairs={{0,2},{1,3},{2,0},{3,1},{4,6},{5,7},{6,4},{7,5},{8,10},{9,11},{10,... | collective-permute-start | bytes 1572872 | tf_op jit(solution)/shard_map/ppermute | solution.py:314
  107.8 11.8 %collective-permute-done.7 = f32[2,2,256,128]{3,2,1,0:T(8,128)S(1)} collective-permute-done((f32[2,2,256,128]{3,2,1,0:T(8,128)S(1)}, f32[2,2,256,128]{3,2,1,0:T(8,128)S(1)}, u32[]{:S(2)}, u32[]{:S(2)}) %collective-permute-start.7) | collective-permute-done | bytes 524320 | tf_op jit(solution)/shard_map/ppermute | solution.py:314
  119.6 0.1 add.10
  119.7 0.8 slice_bitcast_fusion
  120.5 0.0 all-to-all-done.1
  120.6 1.0 copy.13
  (1 shorter events, 0.0 us)
Async XLA Ops:
  0.6 26.1 %copy-start.1 = (f32[2,2,256,256]{3,2,1,0:T(8,128)S(1)}, f32[2,2,256,256]{3,2,1,0:T(8,128)}, u32[]{:S(2)}) copy-start(f32[2,2,256,256]{3,2,1,0:T(8,128)} %probe.1) | copy-start | bytes 3145732
  0.6 7.8 %collective-permute-start = (s32[2,2]{1,0:T(2,128)}, s32[2,2]{1,0:T(2,128)S(1)}, u32[]{:S(2)}, u32[]{:S(2)}) collective-permute-start(s32[2,2]{1,0:T(2,128)} %offsets.7), channel_id=1, source_target_pairs={{0,4},{4,8},{8,12},{12,16},{16,20},{20,24},{24,28},{28,32},{32,36}... | collective-permute-start | bytes 56 | tf_op jit(solution)/shard_map/ppermute | solution.py:286
  4.3 27.2 %collective-permute-start.3 = (f32[2,2,256,256]{3,2,1,0:T(8,128)}, f32[2,2,256,256]{3,2,1,0:T(8,128)S(1)}, u32[]{:S(2)}, u32[]{:S(2)}) collective-permute-start(f32[2,2,256,256]{3,2,1,0:T(8,128)} %probe.1), channel_id=1, source_target_pairs={{0,18},{1,19},{2,16},{3,17},{4,22},{5,23},{6,20},{7,21},{8,26},{9,... | collective-permute-start | bytes 3145736 | tf_op jit(solution)/shard_map/ppermute | solution.py:285
  8.5 1.2 %copy-start.2 = (f32[2,256,512]{2,1,0:T(8,128)S(1)}, f32[2,256,512]{2,1,0:T(8,128)}, u32[]{:S(2)}) copy-start(f32[2,256,512]{2,1,0:T(8,128)} %phase.3) | copy-start | bytes 3145732
  9.7 1.2 %copy-start.3 = (f32[2,256,512]{2,1,0:T(8,128)S(1)}, f32[2,256,512]{2,1,0:T(8,128)}, u32[]{:S(2)}) copy-start(f32[2,256,512]{2,1,0:T(8,128)} %absorb.3) | copy-start | bytes 3145732
  10.9 15.8 %copy-start.5 = (s32[2,2]{1,0:T(2,128)S(1)}, s32[2,2]{1,0:T(2,128)}, u32[]{:S(2)}) copy-start(s32[2,2]{1,0:T(2,128)} %offsets.7) | copy-start | bytes 52
  10.9 20.6 %copy-start.4 = (f32[2,256,512]{2,1,0:T(8,128)S(1)}, f32[2,256,512]{2,1,0:T(8,128)}, u32[]{:S(2)}) copy-start(f32[2,256,512]{2,1,0:T(8,128)} %absorb.3) | copy-start | bytes 3145732
  10.9 20.6 %copy-start.7 = (bf16[6,256,256]{2,1,0:T(8,128)(2,1)S(1)}, bf16[6,256,256]{2,1,0:T(8,128)(2,1)}, u32[]{:S(2)}) copy-start(bf16[6,256,256]{2,1,0:T(8,128)(2,1)} %constant.9.clone.tab_t) | copy-start | bytes 2359300
  10.9 20.6 %copy-start.8 = (bf16[6,256,256]{2,1,0:T(8,128)(2,1)S(1)}, bf16[6,256,256]{2,1,0:T(8,128)(2,1)}, u32[]{:S(2)}) copy-start(bf16[6,256,256]{2,1,0:T(8,128)(2,1)} %constant.8.clone.tab_a) | copy-start | bytes 2359300
  11.5 15.1 %collective-permute-start.1 = (f32[2,2,128,256]{3,2,1,0:T(8,128)S(1)}, f32[2,2,128,256]{3,2,1,0:T(8,128)S(1)}, u32[]{:S(2)}, u32[]{:S(2)}) collective-permute-start(f32[2,2,128,256]{3,2,1,0:T(8,128)S(1)} %shard_map.103), channel_id=1, source_target_pairs={{4,0},{8,4},{12,8},{16,12},{20,16},{24,20},{28,24},{32,28},{36,32}... | collective-permute-start | bytes 1572872 | tf_op jit(solution)/shard_map/ppermute | solution.py:289
  26.7 4.9 %collective-permute-start.2 = (f32[2,2,128,256]{3,2,1,0:T(8,128)S(1)}, f32[2,2,128,256]{3,2,1,0:T(8,128)S(1)}, u32[]{:S(2)}, u32[]{:S(2)}) collective-permute-start(f32[2,2,128,256]{3,2,1,0:T(8,128)S(1)} %collective-permute-done.1.mine), channel_id=1, source_target_pairs={{0,1},{1,0},{2,3},{3,2},{4,5},{5,4},{6,7},{7,6},{8,9},{9,8},{10,11... | collective-permute-start | bytes 1572872 | tf_op jit(solution)/shard_map/ppermute | solution.py:290
  27.7 13.5 %copy-start.6 = (f32[2,256,256]{2,1,0:T(8,128)S(1)}, f32[2,256,256]{2,1,0:T(8,128)}, u32[]{:S(2)}) copy-start(f32[2,256,256]{2,1,0:T(8,128)} %measured.1) | copy-start | bytes 1572868
  39.4 1.8 %collective-permute-start.4 = (f32[256,256]{1,0:T(8,128)S(1)}, f32[256,256]{1,0:T(8,128)S(1)}, u32[]{:S(2)}, u32[]{:S(2)}) collective-permute-start(f32[256,256]{1,0:T(8,128)S(1)} %get-tuple-element.18.power), channel_id=1, source_target_pairs={{0,1},{1,0},{2,3},{3,2},{4,5},{5,4},{6,7},{7,6},{8,9},{9,8},{10,11... | collective-permute-start | bytes 786440 | tf_op jit(solution)/shard_map/ppermute | solution.py:298
  49.9 1.3 %copy-start = (f32[16,2,64,256]{3,2,1,0:T(8,128)}, f32[16,2,64,256]{3,2,1,0:T(8,128)S(1)}, u32[]{:S(2)}) copy-start(f32[16,2,64,256]{3,2,1,0:T(8,128)S(1)} %get-tuple-element.30) | copy-start | bytes 6291460
  51.2 38.0 %all-to-all-start = ((f32[16,2,64,256]{3,2,1,0:T(8,128)}), f32[16,2,64,256]{3,2,1,0:T(8,128)S(1)}, u32[]{:S(2)}, u32[]{:S(2)}) async-start(f32[16,2,64,256]{3,2,1,0:T(8,128)} %copy-done), calls=%async_computation | async-start | bytes 4194304 | tf_op jit(solution)/shard_map/all_to_all | solution.py:317
  58.0 2.0 %collective-permute-start.5 = (f32[2,2,256,128]{3,2,1,0:T(8,128)S(1)}, f32[2,2,256,128]{3,2,1,0:T(8,128)S(1)}, u32[]{:S(2)}, u32[]{:S(2)}) collective-permute-start(f32[2,2,256,128]{3,2,1,0:T(8,128)S(1)} %get-tuple-element.27), channel_id=1, source_target_pairs={{0,1},{1,0},{2,3},{3,2},{4,5},{5,4},{6,7},{7,6},{8,9},{9,8},{10,11... | collective-permute-start | bytes 1572872 | tf_op jit(solution)/shard_map/ppermute | solution.py:311
  60.0 43.9 %collective-permute-start.6 = (f32[2,2,256,128]{3,2,1,0:T(8,128)S(1)}, f32[2,2,256,128]{3,2,1,0:T(8,128)S(1)}, u32[]{:S(2)}, u32[]{:S(2)}) collective-permute-start(f32[2,2,256,128]{3,2,1,0:T(8,128)S(1)} %add.9.pair), channel_id=1, source_target_pairs={{0,4},{4,8},{8,12},{12,16},{16,20},{20,24},{24,28},{28,32},{32,36}... | collective-permute-start | bytes 1572872 | tf_op jit(solution)/shard_map/ppermute | solution.py:312
  89.3 5.6 %collective-permute-start.8 = (f32[64,256]{1,0:T(8,128)S(1)}, f32[64,256]{1,0:T(8,128)S(1)}, u32[]{:S(2)}, u32[]{:S(2)}) collective-permute-start(f32[64,256]{1,0:T(8,128)S(1)} %get-tuple-element.32), channel_id=1, source_target_pairs={{0,18},{1,19},{2,16},{3,17},{4,22},{5,23},{6,20},{7,21},{8,26},{9,... | collective-permute-start | bytes 196616 | tf_op jit(solution)/shard_map/ppermute | solution.py:319
  94.9 4.3 %collective-permute-start.9 = (f32[64,256]{1,0:T(8,128)S(1)}, f32[64,256]{1,0:T(8,128)S(1)}, u32[]{:S(2)}, u32[]{:S(2)}) collective-permute-start(f32[64,256]{1,0:T(8,128)S(1)} %add.11.share), channel_id=1, source_target_pairs={{0,16},{4,20},{8,24},{12,28},{16,0},{20,4},{24,8},{28,12},{32,48},... | collective-permute-start | bytes 196616 | tf_op jit(solution)/shard_map/ppermute | solution.py:320
  100.3 20.2 %all-to-all-start.1 = ((f32[16,64,256]{2,1,0:T(8,128)}), f32[16,64,256]{2,1,0:T(8,128)S(1)}, u32[]{:S(2)}, u32[]{:S(2)}) async-start(f32[16,64,256]{2,1,0:T(8,128)} %shard_map.109), calls=%async_computation.1 | async-start | bytes 2097152 | tf_op jit(solution)/shard_map/all_to_all | solution.py:322
  104.8 14.9 %collective-permute-start.7 = (f32[2,2,256,128]{3,2,1,0:T(8,128)S(1)}, f32[2,2,256,128]{3,2,1,0:T(8,128)S(1)}, u32[]{:S(2)}, u32[]{:S(2)}) collective-permute-start(f32[2,2,256,128]{3,2,1,0:T(8,128)S(1)} %get-tuple-element.29), channel_id=1, source_target_pairs={{0,2},{1,3},{2,0},{3,1},{4,6},{5,7},{6,4},{7,5},{8,10},{9,11},{10,... | collective-permute-start | bytes 1572872 | tf_op jit(solution)/shard_map/ppermute | solution.py:314
